TPU v7x, 256 devices: a whole 4x4x8 slice. The times are simulated.
256 devices in a mesh: group: 8 (over z), mem: 32 (over y, x, core).
Axes of the slice: x: 4, y: 4, z: 8, core: 2. Of those that a mesh axis runs over, the one named last changes fastest.
Arguments:
- memory: float32 [8, 100, 32768], P('group', None, 'mem'), may hold values from -3 to 3
- embedding: bfloat16 [128, 32768], P(None, 'mem'), may hold values from -6 to 6
- owners: int32 [8, 32768, 1], P('group', 'mem'), may hold values from 0 to 31; in each aligned block of 1024 rows (0 to 1023, 1024 to 2047, ..., all dimensions but the last counted through in order) at most 64 rows name the same one
- local_rows: int32 [8, 32768], P('group', 'mem'), may hold values from 0 to 1023
- event_slots: int32 [8, 22, 8192], P('group', None, 'mem'), may hold values from 0 to 1023
- event_ticks: int32 [8, 22, 8192], P('group', None, 'mem'), may hold values from 0 to 999
- w_self: bfloat16 [100, 228], replicated, may hold values from -0.375 to 0.375
- w_neighbour: bfloat16 [100, 228], replicated, may hold values from -0.125 to 0.125
- w_time: bfloat16 [100, 100], replicated, may hold values from -0.1875 to 0.1875
- w_link: bfloat16 [100, 200], replicated, may hold values from -0.4375 to 0.4375
- w_score: bfloat16 [100], replicated, may hold values from -0.625 to 0.625
- w_message: bfloat16 [300, 300], replicated, may hold values from -0.375 to 0.375
- w_hidden: bfloat16 [300, 100], replicated, may hold values from -0.625 to 0.625
- frequencies: float32 [100], replicated, may hold values from 0.001 to 1
- phases: float32 [100], replicated, may hold values from -3.140625 to 3.140625
Outputs:
- new_memory: bfloat16 [8, 100, 32768], P('group', None, 'mem')
- logits: bfloat16 [8, 8192], P('group', 'mem')
Inputs may be any that keep to these rules, and one draw needn't show every extreme that they name: `owners`: at most 64 of the 1024 touched entries of one device name the same owner; in every draw some device names one owner exactly 64 times.
All inputs are finite; a program needn't handle non-finite values.
Results may differ from a plain program's by a relative error of at most 0.018.
Values may be sent and summed in bfloat16 or wider, within the bound.
A program may use at most 128 MiB of HBM per device.

v0:
```python
import jax
import jax.numpy as jnp
from jax import lax
from jax.sharding import PartitionSpec as P


def from_behind(block, axis, distance):
    devices = range(lax.axis_size(axis))
    route = [((i - distance) % len(devices), i) for i in devices]
    return lax.ppermute(block, axis, route)


def local(
    memory,
    embedding,
    owners,
    local_rows,
    event_slots,
    event_ticks,
    w_self,
    w_neighbour,
    w_time,
    w_link,
    w_score,
    w_message,
    w_hidden,
    frequencies,
    phases,
):
    highest = lax.Precision.HIGHEST
    peers = lax.axis_size("mem")
    touch_count = local_rows.shape[1]
    rows_owned = memory.shape[2]
    mem_width = memory.shape[1]
    capacity = 2 * touch_count // peers
    owner_ids = owners[0, :, 0]
    local_ids = local_rows[0]
    member = (owner_ids[:, None] == jnp.arange(peers, dtype=jnp.int32)[None, :]).astype(jnp.int32)
    bucket_rank = jnp.sum((jnp.cumsum(member, axis=0) - 1) * member, axis=1)
    bucket_slot = owner_ids * capacity + bucket_rank
    request = (
        jnp.zeros((peers * capacity,), jnp.int32)
        .at[bucket_slot]
        .set(local_ids)
        .reshape(peers, capacity)
    )
    asked = lax.all_to_all(request, "mem", split_axis=0, concat_axis=0, tiled=True)
    asked_flat = asked.reshape(-1)
    handed = from_behind(memory, "group", 1)[0]
    mem_state = handed.astype(jnp.bfloat16)
    state_rows = jnp.take(mem_state, asked_flat, axis=1).reshape(mem_width, peers, capacity)
    embed_rows = jnp.take(embedding, asked_flat, axis=1).reshape(-1, peers, capacity)
    got_state, got_embed = (
        lax.all_to_all(state_rows, "mem", split_axis=1, concat_axis=1, tiled=True),
        lax.all_to_all(embed_rows, "mem", split_axis=1, concat_axis=1, tiled=True),
    )
    fetched_state = jnp.take(got_state.reshape(mem_width, -1), bucket_slot, axis=1)
    fetched_embed = jnp.take(got_embed.reshape(got_embed.shape[0], -1), bucket_slot, axis=1)
    self_proj = jnp.dot(
        w_self[:, :mem_width], fetched_state, preferred_element_type=jnp.float32
    ) + jnp.dot(w_self[:, mem_width:], fetched_embed, preferred_element_type=jnp.float32)
    neighbour_proj = jnp.dot(
        w_neighbour[:, :mem_width], fetched_state, preferred_element_type=jnp.float32
    ) + jnp.dot(w_neighbour[:, mem_width:], fetched_embed, preferred_element_type=jnp.float32)
    event_refs = event_slots[0]
    event_count = event_refs.shape[1]
    neighbours = (event_refs.shape[0] - 2) // 2
    code_width = frequencies.shape[0]
    tick_values = event_ticks[0].astype(jnp.float32)
    time_codes = jnp.cos(frequencies[:, None, None] * tick_values[None] + phases[:, None, None])
    neighbour_refs = event_refs[2:].reshape(2, neighbours, event_count)
    neighbour_sum = jnp.sum(jnp.take(neighbour_proj, neighbour_refs, axis=1), axis=2)
    code_sum = jnp.sum(time_codes[:, 2:].reshape(code_width, 2, neighbours, event_count), axis=2)
    time_term = jnp.einsum("ht,tse->hse", w_time.astype(jnp.float32), code_sum, precision=highest)
    pre_embed = jnp.take(self_proj, event_refs[:2], axis=1) + neighbour_sum + time_term
    embeds = jax.nn.relu(pre_embed).astype(jnp.bfloat16)
    link_weight = w_link.reshape(w_link.shape[0], 2, -1)
    link = jax.nn.relu(
        jnp.einsum("lsh,hse->le", link_weight, embeds, preferred_element_type=jnp.float32)
    )
    logits = jnp.sum(w_score.astype(jnp.float32)[:, None] * link, axis=0).astype(jnp.bfloat16)
    self_flat = event_refs[:2].reshape(-1)
    other_flat = event_refs[1::-1].reshape(-1)
    target_slot = jnp.take(bucket_slot, self_flat)
    other_state = jnp.take(fetched_state, other_flat, axis=1)
    gap_codes = time_codes[:, :2].reshape(code_width, -1)
    bucket_count = (
        jnp.zeros((1, peers * capacity), jnp.float32)
        .at[0, target_slot]
        .add(1.0)
        .reshape(1, peers, capacity)
    )
    payload = jnp.dot(
        w_message[:, mem_width : 2 * mem_width], other_state, preferred_element_type=jnp.float32
    ) + jnp.dot(w_message[:, 2 * mem_width :].astype(jnp.float32), gap_codes, precision=highest)
    bucket_sum = (
        jnp.zeros((payload.shape[0], peers * capacity), jnp.float32)
        .at[:, target_slot]
        .add(payload)
        .reshape(-1, peers, capacity)
    )
    got_sum, got_count = (
        lax.all_to_all(bucket_sum, "mem", split_axis=1, concat_axis=1, tiled=True),
        lax.all_to_all(bucket_count, "mem", split_axis=1, concat_axis=1, tiled=True),
    )
    owner_sum = (
        jnp.zeros((got_sum.shape[0], rows_owned), jnp.float32)
        .at[:, asked_flat]
        .add(got_sum.reshape(got_sum.shape[0], -1))
    )
    owner_count = jnp.zeros((rows_owned,), jnp.float32).at[asked_flat].add(got_count.reshape(-1))
    own_gate = jnp.dot(w_message[:, :mem_width], mem_state, preferred_element_type=jnp.float32)
    gates_in = (owner_count[None, :] * own_gate + owner_sum) / jnp.maximum(owner_count, 1.0)[
        None, :
    ]
    hidden_in = jnp.dot(w_hidden, mem_state, preferred_element_type=jnp.float32)
    reset = jax.nn.sigmoid(gates_in[:mem_width] + hidden_in[:mem_width])
    update = jax.nn.sigmoid(
        gates_in[mem_width : 2 * mem_width] + hidden_in[mem_width : 2 * mem_width]
    )
    candidate = jnp.tanh(gates_in[2 * mem_width :] + reset * hidden_in[2 * mem_width :])
    updated = (1.0 - update) * candidate + update * handed
    new_memory = jnp.where(owner_count[None, :] > 0.0, updated, handed).astype(jnp.bfloat16)
    return (new_memory[None], logits[None])


def solution(mesh):
    return jax.shard_map(
        local,
        mesh=mesh,
        in_specs=(
            P("group", None, "mem"),
            P(None, "mem"),
            P("group", "mem", None),
            P("group", "mem"),
            P("group", None, "mem"),
            P("group", None, "mem"),
            P(),
            P(),
            P(),
            P(),
            P(),
            P(),
            P(),
            P(),
            P(),
        ),
        out_specs=(P("group", None, "mem"), P("group", "mem")),
        check_vma=False,
    )
```

profile of v0, /device:TPU:1, one launch (start us, length us, event | category | flops | bytes accessed | tf_op | source)
XLA Modules:
  0.0 190.9 jit_solution(1663752255139553623)
XLA Ops:
  0.7 0.7 fusion.29
  1.4 9.0 %reduce-window.6 = s32[32,8,128]{2,1,0:T(8,128)S(1)} reduce-window(s32[32,8,128]{2,1,0:T(8,128)S(1)} %fusion.29, s32[]{:T(128)} %constant.86.clone.1), window={size=1x1x128 pad=0_0x0_0x127_0}, to_apply=%region_0.0 | reduce-window | flops 4161536 | bytes 262148 | tf_op jit(solution)/shard_map/reduce-window
  10.9 0.7 fusion.26
  11.6 0.7 compare_select_fusion.4
  12.3 4.5 %scatter_custom_fusion = s32[2048]{0:T(1024)S(1)} fusion(s32[1024]{0:T(1024)S(1)} %bitcast.133, s32[1024]{0:T(1024)} %bitcast.144, s32[]{:T(128)} %constant.86.clone.1), kind=kCustom, calls=%fused_computation.102 | custom fusion | bytes 8704 | tf_op jit(solution)/shard_map/scatter | solution.py:44
  16.8 0.7 all_to_all.18
  17.5 8.6 %all-to-all-start = ((s32[32,1,64]{2,1,0:T(1,128)}), s32[32,1,64]{2,1,0:T(1,128)S(1)}, u32[]{:S(2)}, u32[]{:S(2)}) async-start(s32[32,1,64]{2,1,0:T(1,128)} %all_to_all.18), calls=%async_computation | async-start | bytes 32768 | tf_op jit(solution)/shard_map/all_to_all | solution.py:47
  26.1 1.8 copy.67
  27.9 1.6 collective-permute-start
  29.6 0.7 compare_and_fusion.3
  30.3 0.8 slice_reduce_fusion
  31.1 0.7 compare_select_fusion.5
  31.7 0.7 slice.67
  32.7 7.5 %add_cosine_fusion = f32[100,22,256]{2,0,1:T(8,128)S(1)} fusion(f32[100]{0:T(128)S(1)} %copy-done.21, f32[22,256]{1,0:T(8,128)S(1)} %bitcast.118, f32[100]{0:T(128)S(1)} %copy-done.22), kind=kLoop, calls=%fused_computation.14 | loop fusion | flops 1126400 | bytes 2276128 | tf_op jit(solution)/shard_map/cos | solution.py:70
  40.5 2.3 %gather_fusion = s32[512]{0:T(512)S(1)} fusion(s32[1024]{0:T(1024)S(1)} %get-tuple-element.3, s32[1024]{0:T(1024)S(1)} %pad_clamp_fusion.2), kind=kCustom, calls=%fused_computation | custom fusion | bytes 6144 | tf_op jit(solution)/shard_map/jit(_take)/gather | solution.py:84
  42.8 2.2 %fusion.30 = f32[512,300]{0,1:T(8,128)} fusion(f32[100,512]{1,0:T(8,128)S(1)} %bitcast.113, bf16[300,300]{1,0:T(8,128)(2,1)} %param.26), kind=kOutput, calls=%fused_computation.67 | convolution fusion | flops 184320000 | bytes 897024 | tf_op jit(solution)/shard_map/dot_general | solution.py:95
  45.0 0.6 compare_and_fusion.2
  45.6 3.3 %scatter_custom_fusion.1 = f32[2048]{0:T(1024)S(1)} fusion(s32[512]{0:T(512)S(1)} %bitcast.142, f32[512]{0:T(512)S(1)} %broadcast.278, f32[]{:T(128)} %constant.85.clone.1), kind=kCustom, calls=%fused_computation.99 | custom fusion | flops 512 | bytes 8196 | tf_op jit(solution)/shard_map/scatter-add | solution.py:90
  48.9 0.7 reshape.349
  49.6 7.7 %all-to-all-start.1 = ((f32[1,32,64]{2,0,1:T(1,128)}), f32[1,32,64]{2,0,1:T(1,128)S(1)}, u32[]{:S(2)}, u32[]{:S(2)}) async-start(f32[1,32,64]{2,0,1:T(1,128)} %reshape.349), calls=%async_computation.1 | async-start | bytes 32768 | tf_op jit(solution)/shard_map/all_to_all | solution.py:104
  57.2 0.5 broadcast.375
  57.7 0.7 reduce.11
  58.6 0.7 copy-done.7
  59.5 6.2 %gather_fusion.1 = bf16[2048,100]{1,0:T(8,128)(2,1)S(1)} fusion(bf16[100,1024]{0,1:T(8,128)(2,1)S(1)} %copy.68, s32[2048]{0:T(1024)S(1)} %broadcast_clamp_fusion.1), kind=kCustom, calls=%fused_computation.1 | custom fusion | bytes 827392 | tf_op jit(solution)/shard_map/jit(_take)/gather | solution.py:51
  65.7 1.1 broadcast_select_fusion.1
  66.8 7.4 %all-to-all-start.2 = ((bf16[100,32,64]{0,2,1:T(8,128)(2,1)}), bf16[100,32,64]{0,2,1:T(8,128)(2,1)S(1)}, u32[]{:S(2)}, u32[]{:S(2)}) async-start(bf16[100,32,64]{0,2,1:T(8,128)(2,1)} %broadcast_select_fusion.1), calls=%async_computation.2 | async-start | bytes 1048576 | tf_op jit(solution)/shard_map/all_to_all | solution.py:54
  74.2 0.6 compare_and_fusion.4
  74.8 1.1 copy.73
  76.0 8.0 %gather_fusion.4 = bf16[2048,128]{1,0:T(8,128)(2,1)} fusion(bf16[128,1024]{0,1:T(8,128)(2,1)S(1)} %copy.73, s32[2048]{0:T(1024)S(1)} %broadcast_clamp_fusion.1), kind=kCustom, calls=%fused_computation.4 | custom fusion | bytes 1056768 | tf_op jit(solution)/shard_map/jit(_take)/gather | solution.py:52
  83.9 2.2 %broadcast_select_fusion = bf16[128,32,64]{0,2,1:T(8,128)(2,1)} fusion(bf16[128,32,64]{0,2,1:T(8,128)(2,1)} %bitcast.111, pred[32,64]{1,0:T(8,128)(4,1)S(1)} %compare_and_fusion.1), kind=kLoop, calls=%fused_computation.32 | loop fusion | flops 262144 | bytes 1050624 | tf_op jit(solution)/shard_map/jit(_take)/select_n | solution.py:52
  86.1 7.4 %all-to-all-start.4 = ((bf16[128,32,64]{0,2,1:T(8,128)(2,1)}), bf16[128,32,64]{0,2,1:T(8,128)(2,1)S(1)}, u32[]{:S(2)}, u32[]{:S(2)}) async-start(bf16[128,32,64]{0,2,1:T(8,128)(2,1)} %broadcast_select_fusion), calls=%async_computation.4 | async-start | bytes 1048576 | tf_op jit(solution)/shard_map/all_to_all | solution.py:55
  93.5 1.5 slice.113
  95.0 2.4 %reduce_sum.41 = f32[100,2,256]{2,0,1:T(8,128)} reduce(f32[100,2,10,256]{3,0,2,1:T(8,128)} %bitcast.110, f32[]{:T(128)} %constant.85.clone.1), dimensions={2}, to_apply=%region_9.10 | reduce | flops 460800 | bytes 2252804 | tf_op jit(solution)/shard_map/reduce_sum | solution.py:73
  97.5 0.6 reshape.362
  98.1 0.5 broadcast.376
  98.7 0.7 reduce.12
  99.4 14.7 %scatter_custom_fusion.2 = f32[1024]{0:T(1024)S(1)} fusion(s32[2048]{0:T(1024)S(1)} %bitcast.122, f32[2048]{0:T(1024)S(1)} %reshape.449, f32[]{:T(128)} %constant.85.clone.1), kind=kCustom, calls=%fused_computation.110 | custom fusion | flops 2048 | bytes 4100 | tf_op jit(solution)/shard_map/scatter-add | solution.py:111
  114.1 3.2 %gather_fusion.2 = bf16[1024,100]{1,0:T(8,128)(2,1)S(1)} fusion(bf16[100,2048]{0,1:T(8,128)(2,1)S(1)} %bitcast.109, s32[1024]{0:T(1024)S(1)} %broadcast_clamp_fusion.2), kind=kCustom, calls=%fused_computation.2 | custom fusion | bytes 413696 | tf_op jit(solution)/shard_map/jit(_take)/gather | solution.py:57
  117.5 1.3 gather_fusion.3
  118.9 0.4 convolution_add_fusion
  119.3 0.3 copy.70
  119.5 5.5 %scatter_custom_fusion.3 = f32[300,2048]{0,1:T(8,128)} fusion(s32[512]{0:T(512)} %bitcast.143, f32[512,300]{1,0:T(8,128)S(1)} %copy.70, f32[]{:T(128)} %constant.85.clone.1), kind=kCustom, calls=%fused_computation.15 | custom fusion | flops 153600 | bytes 2458112 | tf_op jit(solution)/shard_map/scatter-add | solution.py:99
  125.1 7.6 %all-to-all-start.3 = ((f32[300,32,64]{0,2,1:T(8,128)}), f32[300,32,64]{0,2,1:T(8,128)}, u32[]{:S(2)}, u32[]{:S(2)}) async-start(f32[300,32,64]{0,2,1:T(8,128)} %bitcast.108), calls=%async_computation.3 | async-start | bytes 6291456 | tf_op jit(solution)/shard_map/all_to_all | solution.py:103
  132.7 1.4 convolution_multiply_fusion
  134.0 1.8 copy.71
  135.8 1.4 fusion.52
  137.2 3.2 %gather_fusion.5 = bf16[1024,128]{1,0:T(8,128)(2,1)S(1)} fusion(bf16[128,2048]{0,1:T(8,128)(2,1)S(1)} %bitcast.107, s32[1024]{0:T(1024)S(1)} %broadcast_clamp_fusion.2), kind=kCustom, calls=%fused_computation.5 | custom fusion | bytes 528384 | tf_op jit(solution)/shard_map/jit(_take)/gather | solution.py:58
  140.4 0.4 fusion.37
  140.8 0.4 fusion.2
  141.2 0.2 copy.77
  141.4 17.6 %gather_fusion.7 = f32[5120,100]{1,0:T(8,128)} fusion(f32[100,1024]{0,1:T(8,128)S(1)} %copy.77, s32[5120]{0:T(1024)S(1)} %broadcast_clamp_fusion), kind=kCustom, calls=%fused_computation.7 | custom fusion | bytes 4116480 | tf_op jit(solution)/shard_map/jit(_take)/gather | solution.py:72
  159.0 3.0 %select_reduce_fusion = f32[2,256,100]{2,1,0:T(8,128)S(1)} fusion(f32[2,10,256,100]{3,2,1,0:T(8,128)} %bitcast.106, pred[2,10,256]{2,1,0:T(8,128)(4,1)S(1)} %compare_and_fusion), kind=kLoop, calls=%fused_computation.13 | loop fusion | flops 972800 | bytes 2257920 | tf_op jit(solution)/shard_map/reduce_sum | solution.py:72
  162.0 0.8 copy.78
  162.9 0.4 fusion.40
  163.3 0.4 fusion.3
  163.9 1.0 gather_fusion.6
  165.1 0.3 fusion.6
  165.4 0.2 fusion.9
  165.6 0.6 convert_element_type.43
  166.2 5.6 %all-to-all-done.3 = f32[300,32,64]{0,2,1:T(8,128)} async-done(((f32[300,32,64]{0,2,1:T(8,128)}), f32[300,32,64]{0,2,1:T(8,128)}, u32[]{:S(2)}, u32[]{:S(2)}) %all-to-all-start.3) | async-done | bytes 2457632 | tf_op jit(solution)/shard_map/all_to_all | solution.py:103
  171.8 15.1 %scatter_fusion = f32[300,1024]{0,1:T(8,128)S(1)} fusion(f32[300,1024]{0,1:T(8,128)S(1)} %copy.71, s32[2048]{0:T(1024)S(1)} %bitcast.123, f32[2048,300]{1,0:T(8,128)} %bitcast.22), kind=kCustom, calls=%fused_computation.12 | custom fusion | flops 614400 | bytes 7380992 | tf_op jit(solution)/shard_map/scatter-add | solution.py:109
  186.9 1.5 copy.72
  188.4 1.4 broadcast_divide_fusion
  189.9 1.0 fusion.24
  (93 shorter events, 1.9 us)
Async XLA Ops:
  0.6 135.2 %copy-start = (bf16[300,100]{1,0:T(8,128)(2,1)S(1)}, bf16[300,100]{1,0:T(8,128)(2,1)}, u32[]{:S(2)}) copy-start(bf16[300,100]{1,0:T(8,128)(2,1)} %param.27) | copy-start | bytes 180004
  0.6 31.9 %copy-start.17 = (s32[1,22,256]{2,0,1:T(1,128)S(1)}, s32[1,22,256]{2,0,1:T(1,128)}, u32[]{:S(2)}) copy-start(s32[1,22,256]{2,0,1:T(1,128)} %param.20) | copy-start | bytes 67588
  0.7 32.0 %copy-start.22 = (f32[100]{0:T(128)S(1)}, f32[100]{0:T(128)}, u32[]{:S(2)}) copy-start(f32[100]{0:T(128)} %param.28) | copy-start | bytes 1204
  0.7 32.0 %copy-start.21 = (f32[100]{0:T(128)S(1)}, f32[100]{0:T(128)}, u32[]{:S(2)}) copy-start(f32[100]{0:T(128)} %param.29) | copy-start | bytes 1204
  17.5 32.1 %all-to-all-start = ((s32[32,1,64]{2,1,0:T(1,128)}), s32[32,1,64]{2,1,0:T(1,128)S(1)}, u32[]{:S(2)}, u32[]{:S(2)}) async-start(s32[32,1,64]{2,1,0:T(1,128)} %all_to_all.18), calls=%async_computation | async-start | bytes 32768 | tf_op jit(solution)/shard_map/all_to_all | solution.py:47
  27.9 30.6 %collective-permute-start = (f32[1,100,1024]{2,1,0:T(8,128)}, f32[1,100,1024]{2,1,0:T(8,128)S(1)}, u32[]{:S(2)}, u32[]{:S(2)}) collective-permute-start(f32[1,100,1024]{2,1,0:T(8,128)} %copy.67), channel_id=1, source_target_pairs={{224,0},{0,32},{32,64},{64,96},{96,128},{128,160},{160,192},{192,2... | collective-permute-start | bytes 1228808 | tf_op jit(solution)/shard_map/ppermute | solution.py:10
  42.8 15.7 %copy-start.20 = (s32[512,1]{0,1:T(1,128)}, s32[512,1]{0,1:T(1,128)S(1)}, u32[]{:S(2)}) copy-start(s32[512,1]{0,1:T(1,128)S(1)} %compare_select_fusion.7) | copy-start | bytes 6148
  49.6 17.3 %all-to-all-start.1 = ((f32[1,32,64]{2,0,1:T(1,128)}), f32[1,32,64]{2,0,1:T(1,128)S(1)}, u32[]{:S(2)}, u32[]{:S(2)}) async-start(f32[1,32,64]{2,0,1:T(1,128)} %reshape.349), calls=%async_computation.1 | async-start | bytes 32768 | tf_op jit(solution)/shard_map/all_to_all | solution.py:104
  58.6 0.8 copy-start.7
  59.3 7.5 %copy-start.4 = (bf16[100,1024]{1,0:T(8,128)(2,1)}, bf16[100,1024]{1,0:T(8,128)(2,1)S(1)}, u32[]{:S(2)}) copy-start(bf16[100,1024]{1,0:T(8,128)(2,1)S(1)} %bitcast_convert_fusion) | copy-start | bytes 614404
  66.8 19.3 %all-to-all-start.2 = ((bf16[100,32,64]{0,2,1:T(8,128)(2,1)}), bf16[100,32,64]{0,2,1:T(8,128)(2,1)S(1)}, u32[]{:S(2)}, u32[]{:S(2)}) async-start(bf16[100,32,64]{0,2,1:T(8,128)(2,1)} %broadcast_select_fusion.1), calls=%async_computation.2 | async-start | bytes 1048576 | tf_op jit(solution)/shard_map/all_to_all | solution.py:54
  86.1 38.9 %all-to-all-start.4 = ((bf16[128,32,64]{0,2,1:T(8,128)(2,1)}), bf16[128,32,64]{0,2,1:T(8,128)(2,1)S(1)}, u32[]{:S(2)}, u32[]{:S(2)}) async-start(bf16[128,32,64]{0,2,1:T(8,128)(2,1)} %broadcast_select_fusion), calls=%async_computation.4 | async-start | bytes 1048576 | tf_op jit(solution)/shard_map/all_to_all | solution.py:55
  93.5 4.6 %copy-start.23 = (bf16[100]{0:T(256)(128)(2,1)S(1)}, bf16[100]{0:T(256)(128)(2,1)}, u32[]{:S(2)}) copy-start(bf16[100]{0:T(256)(128)(2,1)} %param.25) | copy-start | bytes 604
  95.0 2.5 %copy-start.15 = (bf16[100,200]{0,1:T(8,128)(2,1)S(1)}, bf16[100,200]{0,1:T(8,128)(2,1)}, u32[]{:S(2)}) copy-start(bf16[100,200]{0,1:T(8,128)(2,1)} %param.24) | copy-start | bytes 120004
  97.5 21.4 %copy-start.6 = (f32[512,300]{0,1:T(8,128)S(1)}, f32[512,300]{0,1:T(8,128)}, u32[]{:S(2)}) copy-start(f32[512,300]{0,1:T(8,128)} %fusion.30) | copy-start | bytes 1843204
  97.5 21.4 %copy-start.11 = (bf16[300,300]{1,0:T(8,128)(2,1)S(1)}, bf16[300,300]{1,0:T(8,128)(2,1)}, u32[]{:S(2)}) copy-start(bf16[300,300]{1,0:T(8,128)(2,1)} %param.26) | copy-start | bytes 540004
  97.5 21.4 %copy-start.19 = (pred[512]{0:T(512)(128)(4,1)S(1)}, pred[512]{0:T(512)(128)(4,1)}, u32[]{:S(2)}) copy-start(pred[512]{0:T(512)(128)(4,1)} %compare_and_fusion.4) | copy-start | bytes 1540
  117.3 23.1 %copy-start.2 = (bf16[1024,100]{1,0:T(8,128)(2,1)}, bf16[1024,100]{1,0:T(8,128)(2,1)S(1)}, u32[]{:S(2)}) copy-start(bf16[1024,100]{1,0:T(8,128)(2,1)S(1)} %gather_fusion.2) | copy-start | bytes 614404
  125.1 7.6 %copy-start.5 = (bf16[100,1024]{1,0:T(8,128)(2,1)S(1)}, bf16[100,1024]{1,0:T(8,128)(2,1)}, u32[]{:S(2)}) copy-start(bf16[100,1024]{1,0:T(8,128)(2,1)} %copy-done.4) | copy-start | bytes 614404
  125.1 46.8 %all-to-all-start.3 = ((f32[300,32,64]{0,2,1:T(8,128)}), f32[300,32,64]{0,2,1:T(8,128)}, u32[]{:S(2)}, u32[]{:S(2)}) async-start(f32[300,32,64]{0,2,1:T(8,128)} %bitcast.108), calls=%async_computation.3 | async-start | bytes 6291456 | tf_op jit(solution)/shard_map/all_to_all | solution.py:103
  135.8 4.6 %copy-start.13 = (bf16[100,228]{1,0:T(8,128)(2,1)S(1)}, bf16[100,228]{1,0:T(8,128)(2,1)}, u32[]{:S(2)}) copy-start(bf16[100,228]{1,0:T(8,128)(2,1)} %param.22) | copy-start | bytes 136804
  159.0 3.9 %copy-start.3 = (bf16[1024,100]{1,0:T(8,128)(2,1)S(1)}, bf16[1024,100]{1,0:T(8,128)(2,1)}, u32[]{:S(2)}) copy-start(bf16[1024,100]{1,0:T(8,128)(2,1)} %copy-done.2) | copy-start | bytes 614404
  159.0 3.9 %copy-start.14 = (bf16[100,228]{1,0:T(8,128)(2,1)S(1)}, bf16[100,228]{1,0:T(8,128)(2,1)}, u32[]{:S(2)}) copy-start(bf16[100,228]{1,0:T(8,128)(2,1)} %param.21) | copy-start | bytes 136804
  163.3 1.8 copy-start.9
  163.3 1.8 copy-start.18
  163.3 2.1 %copy-start.12 = (bf16[100,2,100]{0,2,1:T(8,128)(2,1)S(1)}, bf16[100,2,100]{0,2,1:T(8,128)(2,1)}, u32[]{:S(2)}) copy-start(bf16[100,2,100]{0,2,1:T(8,128)(2,1)} %reshape.362) | copy-start | bytes 120004
  163.7 1.4 copy-start.10
  163.7 1.4 copy-start.16
  186.9 2.9 %copy-start.1 = (f32[300,1024]{1,0:T(8,128)S(1)}, f32[300,1024]{1,0:T(8,128)}, u32[]{:S(2)}) copy-start(f32[300,1024]{1,0:T(8,128)} %fusion.52) | copy-start | bytes 3686404
  186.9 2.9 %copy-start.8 = (f32[1,100,1024]{2,1,0:T(8,128)S(1)}, f32[1,100,1024]{2,1,0:T(8,128)}, u32[]{:S(2)}) copy-start(f32[1,100,1024]{2,1,0:T(8,128)} %copy-done.7) | copy-start | bytes 1228804
where the time goes:
time: 193 us; the launch traced here: 191 us
  other arithmetic  72.9 us (38%)
  local copies, waits for them, and re-layouts  63.5 us (33%)
  starting transfers between devices  40.2 us (21%)
  matrix products  7.27 us (4%)
  waiting for transfers between devices  5.65 us (3%)
    gather x1, local copies, waits for them, and re-layouts, local(): jnp.take(neighbour_proj, neighbour_refs, axis=1)  17.6 us
    scatter-add x1, other arithmetic, local(): owner_sum = jnp.zeros((got_sum.shape[0], rows_owned), jnp.float32).at[:,...  15.1 us
    scatter-add x1, other arithmetic, local(): jnp.zeros((rows_owned,), jnp.float32).at[asked_flat]  14.7 us
    another operation x2, other arithmetic  9.04 us
    all_to_all x1, starting transfers between devices, local(): lax.all_to_all(request, 'mem', split_axis=0, concat_axis=0, tiled=True)  8.59 us
    gather x1, local copies, waits for them, and re-layouts, local(): jnp.take(embedding, asked_flat, axis=1).reshape(-1, peers, capacity)  7.98 us
    all_to_all x1, starting transfers between devices, local(): lax.all_to_all(bucket_count, 'mem', split_axis=1, concat_axis=1, tiled=True)  7.66 us
    all_to_all x1, starting transfers between devices, local(): lax.all_to_all(bucket_sum, 'mem', split_axis=1, concat_axis=1, tiled=True)  7.57 us
  transfers between devices with their start and end apart: 6, of which 1 were waited for; matrix products, arithmetic and copies ran while one was open for 56% of the time, Pallas kernels for 0%

commit v1 on v0

v1 whole, which is shorter than its diff:
```python
import jax
import jax.numpy as jnp
from jax import lax
from jax.experimental import pallas as pl
from jax.experimental.pallas import tpu as pltpu
from jax.sharding import PartitionSpec as P

MESH = pl.DeviceIdType.MESH
F32, BF16, I32 = jnp.float32, jnp.bfloat16, jnp.int32
PEERS, CAP, LANES = 32, 64, 128
SLOTS = PEERS * CAP
TURN = 0.15915494309189535
COS = (
    0.9999999890590219,
    -19.739204499453752,
    64.93911745989001,
    -85.45013953080313,
    60.16763095037926,
    -25.96759924649648,
    6.5286581586731725,
)


def nn(a, b):
    return jnp.dot(a, b, preferred_element_type=F32)


def nt(a, b):
    return lax.dot_general(a, b, (((1,), (1,)), ((), ())), preferred_element_type=F32)


def split(x):
    high = x.astype(BF16)
    return high, (x - high.astype(F32)).astype(BF16)


def hot(mask):
    return jnp.where(mask, 1.0, 0.0).astype(BF16)


def iota(shape, dim):
    return lax.broadcasted_iota(I32, shape, dim)


def cos_turns(y):
    r = y - jnp.floor(y + 0.5)
    z = r * r
    acc = jnp.full_like(z, COS[-1])
    for c in COS[-2::-1]:
        acc = acc * z + c
    return acc


def column(row):
    return jnp.broadcast_to(row, (LANES, LANES)).T


def partner(me, d):
    out = 0
    for bit in (1, 2, 4, 8, 16):
        out = out + lax.rem(lax.div(me, bit) + lax.div(d, bit), 2) * bit
    return out


def kernel(
    mem, emb, own, rows, slots, ticks, w_self, w_neigh, w_time, w_link, w_score, w_msg, w_hid, freq, phase,
    new_mem, logits,
    hsend, hrecv, rsend, rrecv, esend, erecv, ssend, srecv, tsend, trecv, msend, mrecv,
    codes, csum, emb_t, mem_t, ask_rows, o_mat, ot_mat, g_mat, gx_mat, p_mat, c_mat, cg_mat,
    wg, wh, wp, base, other_acc, st_acc, ss_acc,
    hsem, send_sem, recv_sem,
):
    me = lax.axis_index("mem")
    group = lax.axis_index("group")
    groups = lax.axis_size("group")
    ahead = lax.rem(group + 1, groups)
    behind = lax.rem(group + groups - 1, groups)
    width, events = 100, slots.shape[2]

    barrier = pltpu.get_barrier_semaphore()
    pl.semaphore_signal(barrier, inc=1, device_id={"group": behind}, device_id_type=MESH)

    def greet(d, c):
        pl.semaphore_signal(barrier, inc=1, device_id={"mem": partner(me, d)}, device_id_type=MESH)
        return c

    lax.fori_loop(1, PEERS, greet, 0)

    def remote(phase_no, src, dst, d):
        return pltpu.make_async_remote_copy(
            src_ref=src.at[d],
            dst_ref=dst.at[d],
            send_sem=send_sem.at[phase_no, d],
            recv_sem=recv_sem.at[phase_no, d],
            device_id={"mem": partner(me, d)},
            device_id_type=MESH,
        )

    def start_all(phase_no, src, dst, low, high):
        def go(d, c):
            remote(phase_no, src, dst, d).start()
            return c

        lax.fori_loop(low, high, go, 0)

    def await_all(phase_no, src, dst, low, high):
        def go(d, c):
            remote(phase_no, src, dst, d).wait_recv()
            return c

        lax.fori_loop(low, high, go, 0)

    for j in range(8):
        block = mem[pl.ds(j, width, stride=8), :]
        hsend[0:width, j * LANES : (j + 1) * LANES] = block.astype(BF16)
    hsend[96:112, :] = jnp.where(iota((16, 1024), 0) < 4, hsend[96:112, :].astype(F32), 0.0).astype(BF16)

    own_rel = own[...] ^ me
    local = rows[...]
    upper = iota((LANES, 2 * LANES), 0)
    lane = iota((LANES, 2 * LANES), 1)
    tri = hot((lane >= LANES) | (upper < lane))
    members = [jnp.where(iota((PEERS, LANES), 0) == own_rel[r : r + 1, :], 1.0, 0.0) for r in range(8)]
    counts = nn(jnp.concatenate(members, axis=0).astype(BF16), tri)
    seen = jnp.zeros((PEERS, LANES), F32)
    ranks = []
    for r in range(8):
        part = counts[r * PEERS : (r + 1) * PEERS, :]
        ranks.append(jnp.sum(members[r] * (part[:, :LANES] + seen), axis=0, keepdims=True))
        seen = seen + part[:, LANES:]
    rank_row = jnp.concatenate(ranks, axis=1)
    own_row = jnp.concatenate([own_rel[r : r + 1, :] for r in range(8)], axis=1)
    local_row = jnp.concatenate([local[r : r + 1, :] for r in range(8)], axis=1)
    rank_int = rank_row.astype(I32)
    in_rank = (iota((LANES, 1024), 0) & (CAP - 1)) == rank_int
    local_low = local_row & 31
    high_part = jnp.where(in_rank, (local_row - local_low).astype(F32), 0.0).astype(BF16)
    low_part = jnp.where(in_rank, local_low.astype(F32), 0.0).astype(BF16)
    member_row = hot(iota((PEERS, 1024), 0) == own_row)
    request = (nt(member_row, high_part) + nt(member_row, low_part)).astype(I32)
    for d in range(PEERS):
        rsend[d] = request[d : d + 1, :]
    rrecv[0] = request[0:1, :]

    pl.semaphore_wait(barrier, PEERS)

    hand = pltpu.make_async_remote_copy(
        src_ref=hsend,
        dst_ref=hrecv,
        send_sem=hsem.at[0],
        recv_sem=hsem.at[1],
        device_id={"group": ahead},
        device_id_type=MESH,
    )
    hand.start()
    start_all(0, rsend, rrecv, 1, PEERS)

    refs = jnp.concatenate([slots[0], slots[1]], axis=1)
    sub8 = iota((16, 1024), 0)
    slot_parts = jnp.where(sub8 == 0, own_row.astype(F32), jnp.where(sub8 == 1, rank_row, 0.0)).astype(BF16)
    picked = nn(slot_parts, hot(iota((1024, 2 * events), 0) == refs))
    end_slot = (picked[0:1, :] * float(CAP) + picked[1:2, :]).astype(I32)
    other_slot = jnp.concatenate([end_slot[:, events:], end_slot[:, :events]], axis=1)

    pad = jnp.zeros((1, LANES - width), F32)
    freq_col = column(jnp.concatenate([freq[...], pad], axis=1) * TURN)[0:104, :]
    phase_col = column(jnp.concatenate([phase[...], pad], axis=1) * TURN)[0:104, :]

    def code(k):
        tick = ticks[k].astype(F32)
        return jnp.concatenate(
            [cos_turns(freq_col * tick[:, h * LANES : (h + 1) * LANES] + phase_col) for h in range(events // LANES)],
            axis=1,
        )

    sub = iota((LANES, 2 * events), 0)
    side = iota((LANES, 2 * events), 1) // events
    ends = jnp.concatenate([code(0), code(1)], axis=1)
    ends = jnp.concatenate([ends, jnp.zeros((LANES - 104, 2 * events), F32)], axis=0)
    codes[...] = jnp.where(sub < width, ends, jnp.where(sub == width + side, 1.0, 0.0)).astype(BF16)

    def time_chunk(q, c):
        at = pl.multiple_of(q * 512, 512)
        block = hot(iota((512, 2 * events), 0) + at == end_slot)
        g_mat[pl.ds(at, 512), :] = block
        sums = nt(block, codes[...]).astype(BF16)
        for i in range(8):
            tsend[q * 8 + i] = sums[i * CAP : (i + 1) * CAP, :]
        return c

    lax.fori_loop(0, 4, time_chunk, 0)
    trecv[0] = tsend[0]
    start_all(1, tsend, trecv, 1, PEERS)

    emb_t[...] = emb[...].T

    await_all(0, rsend, rrecv, 1, PEERS)
    for p in range(PEERS // 2):
        pair = jnp.where(iota((1, LANES), 1) < CAP, rrecv[2 * p], rrecv[2 * p + 1])
        ask_rows[p] = pair

    def ask_chunk(p, c):
        asked = column(ask_rows[p].astype(F32)).astype(I32)
        at = pl.multiple_of(p * LANES, LANES)
        for j in range(8):
            o_mat[pl.ds(at, LANES), j * LANES : (j + 1) * LANES] = hot(iota((LANES, LANES), 1) + j * LANES == asked)
        return c

    lax.fori_loop(0, PEERS // 2, ask_chunk, 0)

    hand.wait_recv()
    mem_t[:, 0:112] = hrecv[...].astype(F32).T.astype(BF16)
    mem_t[:, 112:128] = jnp.zeros((1024, 16), BF16)

    def serve(phase_no, table, src, dst):
        def chunk(q, c):
            at = pl.multiple_of(q * 512, 512)
            got = nn(o_mat[pl.ds(at, 512), :], table[...]).astype(BF16)
            for i in range(8):
                src[q * 8 + i] = got[i * CAP : (i + 1) * CAP, :]
            start_all(phase_no, src, dst, jnp.maximum(q * 8, 1), q * 8 + 8)
            return c

        lax.fori_loop(0, 4, chunk, 0)
        dst[0] = src[0]

    serve(2, mem_t, ssend, srecv)
    serve(3, emb_t, esend, erecv)

    wg[...] = jnp.zeros_like(wg)
    wh[...] = jnp.zeros_like(wh)
    wp[...] = jnp.zeros_like(wp)
    for gate in range(3):
        for part in range(3):
            wg[gate, part, 0:width, 0:width] = w_msg[
                gate * width : (gate + 1) * width, part * width : (part + 1) * width
            ]
        wh[gate, 0:width, 0:width] = w_hid[gate * width : (gate + 1) * width, :]
    for which, w in enumerate((w_self, w_neigh)):
        wp[which, 0, 0:width, 0:width] = w[:, 0:width]
        wp[which, 1, 0:width, :] = w[:, width:]

    for gate in range(3):
        hidden = nt(wh[gate], mem_t[...])
        own_part = nt(wg[gate, 0], mem_t[...])
        if gate < 2:
            base[gate] = hidden + own_part
        else:
            base[2] = own_part
            base[3] = hidden

    def turn_chunk(j, c):
        at = pl.multiple_of(j * LANES, LANES)
        ask = jnp.concatenate([ask_rows[p] for p in range(PEERS // 2)], axis=1)
        ot_mat[pl.ds(at, LANES), :] = hot(iota((LANES, SLOTS), 0) + at == ask)
        return c

    lax.fori_loop(0, 8, turn_chunk, 0)

    for m in range(2 * events // LANES):
        col = column(other_slot[:, m * LANES : (m + 1) * LANES].astype(F32)).astype(I32)

        def gx_chunk(j, c, col=col, m=m):
            at = pl.multiple_of(j * LANES, LANES)
            gx_mat[m * LANES : (m + 1) * LANES, pl.ds(at, LANES)] = hot(iota((LANES, LANES), 1) + at == col)
            return c

        lax.fori_loop(0, SLOTS // LANES, gx_chunk, 0)

    neighbours = (slots.shape[0] - 2) // 2

    def count_chunk(q, c):
        at = pl.multiple_of(q * CAP, CAP)
        index = iota((CAP, events), 0) + at
        for s in range(2):
            total = jnp.zeros((CAP, events), F32)
            for j in range(neighbours):
                total = total + jnp.where(index == slots[2 + s * neighbours + j], 1.0, 0.0)
            c_mat[pl.ds(at, CAP), s * events : (s + 1) * events] = total.astype(BF16)
        return c

    lax.fori_loop(0, 1024 // CAP, count_chunk, 0)
    slot_row = own_row * CAP + rank_int

    def spread_chunk(q, c):
        at = pl.multiple_of(q * 512, 512)
        p_mat[...] = hot(iota((512, 1024), 0) + at == slot_row)
        cg_mat[pl.ds(at, 512), :] = nn(p_mat[...], c_mat[...]).astype(BF16)
        return c

    lax.fori_loop(0, 4, spread_chunk, 0)

    other_acc[...] = jnp.zeros_like(other_acc)

    def other_chunk(q, c):
        await_all(2, ssend, srecv, jnp.maximum(q * 8, 1), q * 8 + 8)
        at = pl.multiple_of(q * 512, 512)
        block = srecv[pl.ds(pl.multiple_of(q * 8, 8), 8)].reshape(512, LANES)
        other_acc[...] += nn(gx_mat[:, pl.ds(at, 512)], block)
        return c

    lax.fori_loop(0, 4, other_chunk, 0)
    other_state = other_acc[...].astype(BF16)

    def state_chunk(q, c):
        at = pl.multiple_of(q * 512, 512)
        sums = nn(g_mat[pl.ds(at, 512), :], other_state).astype(BF16)
        for i in range(8):
            msend[q * 8 + i] = sums[i * CAP : (i + 1) * CAP, :]
        start_all(4, msend, mrecv, jnp.maximum(q * 8, 1), q * 8 + 8)
        return c

    lax.fori_loop(0, 4, state_chunk, 0)
    mrecv[0] = msend[0]

    for s in range(2):
        def add_code(j, total, s=s):
            return total + code(2 + s * neighbours + j)

        csum[:, s * events : (s + 1) * events] = lax.fori_loop(
            0, neighbours, add_code, jnp.zeros((104, events), F32)
        )

    await_all(1, tsend, trecv, 1, PEERS)
    st_acc[...] = nn(ot_mat[...], trecv[...].reshape(SLOTS, LANES))

    await_all(3, esend, erecv, 1, PEERS)
    state_all = srecv[...].reshape(SLOTS, LANES)
    embed_all = erecv[...].reshape(SLOTS, LANES)
    pre = jnp.zeros((112, 2 * events), F32)
    for which, table in enumerate((g_mat, cg_mat)):
        proj = nt(wp[which, 0], state_all) + nt(wp[which, 1], embed_all)
        high, low = split(proj)
        pre = pre + nn(high, table[...]) + nn(low, table[...])
    high, low = split(csum[0:width, :])
    embeds = pre[0:width, :] + nn(w_time[...], high) + nn(w_time[...], low)
    embeds = jnp.maximum(embeds, 0.0).astype(BF16)
    link = nn(w_link[:, 0:width], embeds[:, :events]) + nn(w_link[:, width:], embeds[:, events:])
    high, low = split(jnp.maximum(link, 0.0))
    score = jnp.broadcast_to(w_score[...], (16, width))
    logits[...] = (nn(score, high) + nn(score, low))[0:1, :].astype(BF16)

    ss_acc[...] = jnp.zeros_like(ss_acc)

    def sum_chunk(q, c):
        await_all(4, msend, mrecv, jnp.maximum(q * 8, 1), q * 8 + 8)
        at = pl.multiple_of(q * 512, 512)
        block = mrecv[pl.ds(pl.multiple_of(q * 8, 8), 8)].reshape(512, LANES)
        ss_acc[...] += nn(ot_mat[:, pl.ds(at, 512)], block)
        return c

    lax.fori_loop(0, 4, sum_chunk, 0)

    t_high, t_low = split(st_acc[...])
    s_high, s_low = split(ss_acc[...])
    lane16 = iota((16, LANES), 1)
    tally = hot((iota((16, LANES), 0) == 0) & ((lane16 == width) | (lane16 == width + 1)))
    count = (nt(tally, t_high) + nt(tally, t_low))[0:1, :]
    inverse = 1.0 / jnp.maximum(count, 1.0)

    def messages(gate):
        ws, wt = wg[gate, 1], wg[gate, 2]
        return (nt(ws, s_high) + nt(ws, s_low) + nt(wt, t_high) + nt(wt, t_low)) * inverse

    reset = jax.nn.sigmoid(base[0] + messages(0))
    update = jax.nn.sigmoid(base[1] + messages(1))
    candidate = jnp.tanh(base[2] + messages(2) + reset * base[3])
    handed = hrecv[...].astype(F32)
    updated = (1.0 - update) * candidate + update * handed
    new_mem[...] = jnp.where(count > 0.0, updated, handed)[0:width, :].astype(BF16)

    hand.wait_send()

    def drain(d, c):
        for phase_no, src, dst in (
            (0, rsend, rrecv), (1, tsend, trecv), (2, ssend, srecv), (3, esend, erecv), (4, msend, mrecv),
        ):
            remote(phase_no, src, dst, d).wait_send()
        return c

    lax.fori_loop(1, PEERS, drain, 0)


def local_step(
    memory, embedding, owners, local_rows, event_slots, event_ticks,
    w_self, w_neighbour, w_time, w_link, w_score, w_message, w_hidden, frequencies, phases,
):
    nodes = memory.shape[2]
    events = event_slots.shape[2]
    args = (
        memory.reshape(-1, LANES),
        embedding,
        owners.reshape(-1, LANES),
        local_rows.reshape(-1, LANES),
        event_slots.transpose(1, 0, 2),
        event_ticks.transpose(1, 0, 2),
        w_self,
        w_neighbour,
        w_time,
        w_link,
        w_score.reshape(1, -1),
        w_message,
        w_hidden,
        frequencies.reshape(1, -1),
        phases.reshape(1, -1),
    )
    vmem = pl.BlockSpec(memory_space=pltpu.VMEM)
    block = (PEERS, CAP, LANES)
    scratch = [
        pltpu.VMEM((112, nodes), BF16),
        pltpu.VMEM((112, nodes), BF16),
        pltpu.VMEM((PEERS, 1, LANES), I32),
        pltpu.VMEM((PEERS, 1, LANES), I32),
        *[pltpu.VMEM(block, BF16)] * 8,
        pltpu.VMEM((LANES, 2 * events), BF16),
        pltpu.VMEM((104, 2 * events), F32),
        pltpu.VMEM((nodes, LANES), BF16),
        pltpu.VMEM((nodes, LANES), BF16),
        pltpu.VMEM((PEERS // 2, 1, LANES), I32),
        pltpu.VMEM((SLOTS, nodes), BF16),
        pltpu.VMEM((nodes, SLOTS), BF16),
        pltpu.VMEM((SLOTS, 2 * events), BF16),
        pltpu.VMEM((2 * events, SLOTS), BF16),
        pltpu.VMEM((512, 1024), BF16),
        pltpu.VMEM((1024, 2 * events), BF16),
        pltpu.VMEM((SLOTS, 2 * events), BF16),
        pltpu.VMEM((3, 3, 112, LANES), BF16),
        pltpu.VMEM((3, 112, LANES), BF16),
        pltpu.VMEM((2, 2, 112, LANES), BF16),
        pltpu.VMEM((4, 112, nodes), F32),
        pltpu.VMEM((2 * events, LANES), F32),
        pltpu.VMEM((nodes, LANES), F32),
        pltpu.VMEM((nodes, LANES), F32),
        pltpu.SemaphoreType.DMA((2,)),
        pltpu.SemaphoreType.DMA((5, PEERS)),
        pltpu.SemaphoreType.DMA((5, PEERS)),
    ]
    new_memory, logits = pl.pallas_call(
        kernel,
        out_shape=(
            jax.ShapeDtypeStruct((memory.shape[1], nodes), BF16),
            jax.ShapeDtypeStruct((1, events), BF16),
        ),
        in_specs=[vmem] * len(args),
        out_specs=(vmem, vmem),
        scratch_shapes=scratch,
        compiler_params=pltpu.CompilerParams(
            collective_id=0, has_side_effects=True, vmem_limit_bytes=56 * 1024 * 1024
        ),
    )(*args)
    return new_memory[None], logits


def solution(mesh):
    return jax.shard_map(
        local_step,
        mesh=mesh,
        in_specs=(
            P("group", None, "mem"),
            P(None, "mem"),
            P("group", "mem", None),
            P("group", "mem"),
            P("group", None, "mem"),
            P("group", None, "mem"),
            P(),
            P(),
            P(),
            P(),
            P(),
            P(),
            P(),
            P(),
            P(),
        ),
        out_specs=(P("group", None, "mem"), P("group", "mem")),
        check_vma=False,
    )
```

time: 193 us -> 55.5 us (0.29)
  other arithmetic: 72.9 us -> 0 us
  local copies, waits for them, and re-layouts: 63.5 us -> 3.73 us
  Pallas kernels: 0 us -> 51 us
  starting transfers between devices: 40.2 us -> 0 us
  matrix products: 7.27 us -> 0 us
  waiting for transfers between devices: 5.65 us -> 0 us
    pallas_call x0 -> x1, Pallas kernels: none -> 51 us  [local_step(): pl.pallas_call(kernel, out_shape=(jax.ShapeDtypeStruct((memory.shape[1],...]
    gather x9 -> x0, local copies, waits for them, and re-layouts: 43 us -> none  [the longest x1 17.6 us: local(): jnp.take(neighbour_proj, neighbour_refs, axis=1)]
    all_to_all x5 -> x0, starting transfers between devices: 38.6 us -> none  [the longest x1 8.59 us: local(): lax.all_to_all(request, 'mem', split_axis=0, concat_axis=0, tiled=True)]
    scatter-add x4 -> x0, other arithmetic: 38.5 us -> none  [the longest x1 15.1 us: local(): owner_sum = jnp.zeros((got_sum.shape[0], rows_owned), jnp.float32).at[:,...]
    another operation x2 -> x0, other arithmetic: 9.04 us -> none
    cos x1 -> x0, other arithmetic: 7.55 us -> none  [local(): jnp.cos(frequencies[:, None, None] * tick_values[None] + phases[:, None,...]
    dot_general x10 -> x0, matrix products: 7.27 us -> none  [the longest x1 2.19 us: local(): jnp.dot(w_message[:, 2 * mem_width:].astype(jnp.float32), gap_codes, prec...]
    reduce_sum x3 -> x0, other arithmetic: 6.19 us -> none  [the longest x1 3.02 us: local(): jnp.sum(jnp.take(neighbour_proj, neighbour_refs, axis=1), axis=2)]
  transfers between devices with their start and end apart: 6 -> 0, of which waited for: 1 -> 0; matrix products, arithmetic and copies ran while one was open for 56% -> 0% of each run, Pallas kernels for 0% -> 0%
where the time goes in v1:
time: 55.5 us; the launch traced here: 55.3 us
  Pallas kernels  51 us (92%)
  local copies, waits for them, and re-layouts  3.73 us (7%)
  between operations  0.65 us (1%)
    pallas_call x1, Pallas kernels, local_step(): pl.pallas_call(kernel, out_shape=(jax.ShapeDtypeStruct((memory.shape[1],...  51 us
    unnamed x5, local copies, waits for them, and re-layouts  3.73 us

profile of v1, /device:TPU:1, one launch (start us, length us, event | category | flops | bytes accessed | tf_op | source)
XLA Modules:
  0.0 55.3 jit_solution(6017928258468306182)
XLA Ops:
  0.6 1.5 %copy.17.w_link = bf16[100,200]{1,0:T(8,128)(2,1)} copy(bf16[100,200]{0,1:T(8,128)(2,1)} %param.24) | data formatting | bytes 80000 | tf_op args[9]
  2.2 51.0 %shard_map.158 = (bf16[100,1024]{1,0:T(8,128)(2,1)}, bf16[1,256]{1,0:T(2,128)(2,1)}) custom-call(f32[800,128]{1,0:T(8,128)} %bitcast.9, bf16[128,1024]{1,0:T(8,128)(2,1)} %emb.1, s32[8,128]{1,0:T(8,128)} %bitcast.13, s32[8,128]{1,0:T(8,128)} %bitcast.14, s32[22,1,256]{2,1,0:T(1,128)} %bitcast.11, s32[22,1,256]{2,1,0:T(1,128)} %bitcast.12, ...), custom_call_target="tpu_custom_call" | custom-call | tf_op jit(solution)/shard_map/pallas_call | solution.py:438
  53.1 0.0 copy-start
  53.1 1.6 %copy.20 = bf16[1,100,1024]{2,1,0:T(8,128)(2,1)} copy(bf16[1,100,1024]{2,1,0:T(8,128)(2,1)} %bitcast.10) | data formatting | bytes 409600
  54.8 0.0 copy-done
  54.8 0.6 %copy.21 = bf16[1,256]{1,0:T(2,128)(2,1)} copy(bf16[1,256]{1,0:T(2,128)(2,1)S(1)} %copy-done) | data formatting | bytes 1024
Async XLA Ops:
  53.1 1.6 %copy-start = (bf16[1,256]{1,0:T(2,128)(2,1)S(1)}, bf16[1,256]{1,0:T(2,128)(2,1)}, u32[]{:S(2)}) copy-start(bf16[1,256]{1,0:T(2,128)(2,1)} %get-tuple-element.9) | copy-start | bytes 1540

commit v2 on v1

v2 whole, which is shorter than its diff:
```python
import jax
import jax.numpy as jnp
from jax import lax
from jax.experimental import pallas as pl
from jax.experimental.pallas import tpu as pltpu
from jax.sharding import PartitionSpec as P

MESH = pl.DeviceIdType.MESH
F32, BF16, I32, I16 = jnp.float32, jnp.bfloat16, jnp.int32, jnp.int16
PEERS, CAP, LANES = 32, 64, 128
SLOTS = PEERS * CAP
TURN = 0.15915494309189535
COS = (
    0.9999999890590219,
    -19.739204499453752,
    64.93911745989001,
    -85.45013953080313,
    60.16763095037926,
    -25.96759924649648,
    6.5286581586731725,
)


def nn(a, b):
    return jnp.dot(a, b, preferred_element_type=F32)


def nt(a, b):
    return lax.dot_general(a, b, (((1,), (1,)), ((), ())), preferred_element_type=F32)


def split(x):
    high = x.astype(BF16)
    return high, (x - high.astype(F32)).astype(BF16)


def hot(mask):
    return jnp.where(mask, 1.0, 0.0).astype(BF16)


def iota(shape, dim):
    return lax.broadcasted_iota(I32, shape, dim)


def tn(a, b):
    return lax.dot_general(a, b, (((0,), (0,)), ((), ())), preferred_element_type=F32)


def sigmoid(x):
    return 0.5 * jnp.tanh(0.5 * x) + 0.5


def hot_rows(row, count):
    shape = (16, row.shape[1])
    named = jnp.broadcast_to(row, shape).astype(I16)
    index = iota(shape, 0).astype(I16)
    one, zero = jnp.ones(shape, BF16), jnp.zeros(shape, BF16)
    return jnp.concatenate([jnp.where(index + jnp.int16(i) == named, one, zero) for i in range(0, count, 16)], axis=0)


def cos_turns(y):
    r = y - jnp.floor(y + 0.5)
    z = r * r
    acc = jnp.full_like(z, COS[-1])
    for c in COS[-2::-1]:
        acc = acc * z + c
    return acc


def column(row):
    return jnp.broadcast_to(row, (LANES, LANES)).T


def partner(me, d):
    out = 0
    for bit in (1, 2, 4, 8, 16):
        out = out + lax.rem(lax.div(me, bit) + lax.div(d, bit), 2) * bit
    return out


def kernel(
    mem, emb, own, rows, slots, ticks, w_self, w_neigh, w_time, w_link, w_score, w_msg, w_hid, freq, phase,
    new_mem, logits,
    hsend, hrecv, rsend, rrecv, esend, erecv, ssend, srecv, tsend, trecv, msend, mrecv,
    codes, csum, table, o_mat, g_mat, p_mat, c_mat,
    wg, wh, wp, base, time_part, self_acc, t_acc, s_acc,
    hsem, send_sem, recv_sem,
):
    me = lax.axis_index("mem")
    group = lax.axis_index("group")
    groups = lax.axis_size("group")
    ahead = lax.rem(group + 1, groups)
    behind = lax.rem(group + groups - 1, groups)
    width, events = 100, slots.shape[2]

    barrier = pltpu.get_barrier_semaphore()
    pl.semaphore_signal(barrier, inc=1, device_id={"group": behind}, device_id_type=MESH)

    def greet(d, c):
        pl.semaphore_signal(barrier, inc=1, device_id={"mem": partner(me, d)}, device_id_type=MESH)
        return c

    lax.fori_loop(1, PEERS, greet, 0)

    def remote(phase_no, src, dst, d):
        return pltpu.make_async_remote_copy(
            src_ref=src.at[d],
            dst_ref=dst.at[d],
            send_sem=send_sem.at[phase_no, d],
            recv_sem=recv_sem.at[phase_no, d],
            device_id={"mem": partner(me, d)},
            device_id_type=MESH,
        )

    def start_all(phase_no, src, dst, low, high):
        def go(d, c):
            remote(phase_no, src, dst, d).start()
            return c

        lax.fori_loop(low, high, go, 0)

    def await_all(phase_no, src, dst, low, high):
        def go(d, c):
            remote(phase_no, src, dst, d).wait_recv()
            return c

        lax.fori_loop(low, high, go, 0)

    for j in range(8):
        block = mem[pl.ds(j, width, stride=8), :]
        hsend[0:width, j * LANES : (j + 1) * LANES] = block.astype(BF16)
    hsend[96:112, :] = jnp.where(iota((16, 1024), 0) < 4, hsend[96:112, :].astype(F32), 0.0).astype(BF16)

    own_rel = own[...] ^ me
    local = rows[...]
    upper = iota((LANES, 2 * LANES), 0)
    lane = iota((LANES, 2 * LANES), 1)
    tri = hot((lane >= LANES) | (upper < lane))
    members = [jnp.where(iota((PEERS, LANES), 0) == own_rel[r : r + 1, :], 1.0, 0.0) for r in range(8)]
    counts = nn(jnp.concatenate(members, axis=0).astype(BF16), tri)
    seen = jnp.zeros((PEERS, LANES), F32)
    ranks = []
    for r in range(8):
        part = counts[r * PEERS : (r + 1) * PEERS, :]
        ranks.append(jnp.sum(members[r] * (part[:, :LANES] + seen), axis=0, keepdims=True))
        seen = seen + part[:, LANES:]
    rank_row = jnp.concatenate(ranks, axis=1)
    own_row = jnp.concatenate([own_rel[r : r + 1, :] for r in range(8)], axis=1)
    local_row = jnp.concatenate([local[r : r + 1, :] for r in range(8)], axis=1)
    rank_int = rank_row.astype(I32)
    in_rank = (iota((LANES, 1024), 0) & (CAP - 1)) == rank_int
    local_low = local_row & 31
    high_part = jnp.where(in_rank, (local_row - local_low).astype(F32), 0.0).astype(BF16)
    low_part = jnp.where(in_rank, local_low.astype(F32), 0.0).astype(BF16)
    member_row = hot_rows(own_row, PEERS)
    request = (nt(member_row, high_part) + nt(member_row, low_part)).astype(I32)
    for d in range(PEERS):
        rsend[d] = request[d : d + 1, :]
    rrecv[0] = request[0:1, :]

    refs = jnp.concatenate([slots[0], slots[1]], axis=1)
    sub8 = iota((16, 1024), 0)
    slot_parts = jnp.where(sub8 == 0, own_row.astype(F32), jnp.where(sub8 == 1, rank_row, 0.0)).astype(BF16)
    picked = nn(slot_parts, hot_rows(refs, 1024))
    end_slot = (picked[0:1, :] * float(CAP) + picked[1:2, :]).astype(I32)
    g_mat[...] = hot_rows(end_slot, SLOTS)

    pad = jnp.zeros((1, LANES - width), F32)
    freq_col = column(jnp.concatenate([freq[...], pad], axis=1) * TURN)[0:104, :]
    phase_col = column(jnp.concatenate([phase[...], pad], axis=1) * TURN)[0:104, :]

    def code(k):
        tick = ticks[k].astype(F32)
        return jnp.concatenate(
            [cos_turns(freq_col * tick[:, h * LANES : (h + 1) * LANES] + phase_col) for h in range(events // LANES)],
            axis=1,
        )

    sub = iota((LANES, 2 * events), 0)
    side = iota((LANES, 2 * events), 1) // events
    ends = jnp.concatenate([code(0), code(1)], axis=1)
    ends = jnp.concatenate([ends, jnp.zeros((LANES - 104, 2 * events), F32)], axis=0)
    codes[...] = jnp.where(sub < width, ends, jnp.where(sub == width + side, 1.0, 0.0)).astype(BF16)

    sums = nt(g_mat[...], codes[...]).astype(BF16)
    for d in range(PEERS):
        tsend[d] = sums[d * CAP : (d + 1) * CAP, :]
    trecv[0] = tsend[0]
    table[:, LANES:] = emb[...].T

    pl.semaphore_wait(barrier, PEERS)

    hand = pltpu.make_async_remote_copy(
        src_ref=hsend,
        dst_ref=hrecv,
        send_sem=hsem.at[0],
        recv_sem=hsem.at[1],
        device_id={"group": ahead},
        device_id_type=MESH,
    )
    hand.start()
    start_all(0, rsend, rrecv, 1, PEERS)
    start_all(1, tsend, trecv, 1, PEERS)

    wg[...] = jnp.zeros_like(wg)
    wh[...] = jnp.zeros_like(wh)
    wp[...] = jnp.zeros_like(wp)
    for gate in range(3):
        for part in range(3):
            wg[part, gate * 112 : gate * 112 + width, 0:width] = w_msg[
                gate * width : (gate + 1) * width, part * width : (part + 1) * width
            ]
        wh[gate * 112 : gate * 112 + width, 0:width] = w_hid[gate * width : (gate + 1) * width, :]
    tally_lane = iota((16, LANES), 1)
    tally = (iota((16, LANES), 0) == 0) & ((tally_lane == width) | (tally_lane == width + 1))
    wg[2, 336:352, :] = hot(tally)
    for which, w in enumerate((w_self, w_neigh)):
        wp[which, 0:width, 0:width] = w[:, 0:width]
        wp[which, 0:width, LANES:] = w[:, width:]

    neighbours = (slots.shape[0] - 2) // 2
    one, zero = jnp.ones((16, 2 * events), BF16), jnp.zeros((16, 2 * events), BF16)
    index16 = iota((16, 2 * events), 0).astype(I16)
    near = [
        jnp.broadcast_to(jnp.concatenate([slots[2 + j], slots[2 + neighbours + j]], axis=1), one.shape).astype(I16)
        for j in range(neighbours)
    ]
    for q in range(64):
        total = zero
        index = index16 + jnp.int16(q * 16)
        for j in range(neighbours):
            total = total + jnp.where(index == near[j], one, zero)
        c_mat[q * 16 : (q + 1) * 16, :] = total
    p_mat[...] = hot_rows(own_row * CAP + rank_int, SLOTS)

    for s in range(2):
        def add_code(j, total, s=s):
            return total + code(2 + s * neighbours + j)

        csum[:, s * events : (s + 1) * events] = lax.fori_loop(
            0, neighbours, add_code, jnp.zeros((104, events), F32)
        )

    await_all(0, rsend, rrecv, 1, PEERS)
    for p in range(PEERS // 2):
        pair = jnp.where(iota((1, LANES), 1) < CAP, rrecv[2 * p], rrecv[2 * p + 1])
        asked = column(pair.astype(F32)).astype(I32).astype(I16)
        for j in range(8):
            index = (iota((LANES, LANES), 1) + j * LANES).astype(I16)
            o_mat[p * LANES : (p + 1) * LANES, j * LANES : (j + 1) * LANES] = jnp.where(
                index == asked, jnp.ones((LANES, LANES), BF16), jnp.zeros((LANES, LANES), BF16)
            )
    hand.wait_recv()
    table[:, 0:112] = hrecv[...].T
    table[:, 112:128] = jnp.zeros((1024, 16), BF16)
    for q in range(4):
        got = nn(o_mat[q * 512 : (q + 1) * 512, :], table[...]).astype(BF16)
        for i in range(8):
            ssend[q * 8 + i] = got[i * CAP : (i + 1) * CAP, :LANES]
            esend[q * 8 + i] = got[i * CAP : (i + 1) * CAP, LANES:]
        start_all(2, ssend, srecv, max(q * 8, 1), q * 8 + 8)
    start_all(3, esend, erecv, 1, PEERS)
    srecv[0] = ssend[0]
    erecv[0] = esend[0]

    base[0:336, :] = nn(wg[0, 0:336, 0:112], hrecv[...])
    hidden = nn(wh[...], hrecv[...])
    base[0:224, :] = base[0:224, :] + hidden[0:224, :]
    base[336:448, :] = hidden[224:336, :]

    for q in range(4):
        await_all(2, ssend, srecv, max(q * 8, 1), q * 8 + 8)
        block = srecv[q * 8 : (q + 1) * 8].reshape(512, LANES)
        part = tn(block, g_mat[q * 512 : (q + 1) * 512, :])
        self_acc[...] = part if q == 0 else self_acc[...] + part
    self_state = self_acc[...].astype(BF16)
    other_state = jnp.concatenate([self_state[:, events:], self_state[:, :events]], axis=1)
    for q in range(4):
        sums = nt(g_mat[q * 512 : (q + 1) * 512, :], other_state).astype(BF16)
        for i in range(8):
            msend[q * 8 + i] = sums[i * CAP : (i + 1) * CAP, :]
        start_all(4, msend, mrecv, max(q * 8, 1), q * 8 + 8)
    mrecv[0] = msend[0]

    await_all(1, tsend, trecv, 1, PEERS)
    t_acc[...] = tn(trecv[...].reshape(SLOTS, LANES), o_mat[...]).astype(BF16)
    time_part[...] = nn(wg[2], t_acc[...])

    await_all(3, esend, erecv, 1, PEERS)
    embed_all = erecv[...].reshape(SLOTS, LANES)
    fetched_state = tn(srecv[...].reshape(SLOTS, LANES), p_mat[...]).astype(BF16)
    fetched_embed = tn(embed_all, p_mat[...]).astype(BF16)
    near_state = nn(fetched_state, c_mat[...])
    near_embed = nn(fetched_embed, c_mat[...])
    self_embed = tn(embed_all, g_mat[...]).astype(BF16)
    pre = nn(wp[0], jnp.concatenate([self_state, self_embed], axis=0))
    for half in split(jnp.concatenate([near_state, near_embed], axis=0)):
        pre = pre + nn(wp[1], half)
    high, low = split(csum[0:width, :])
    embeds = pre[0:width, :] + nn(w_time[...], high) + nn(w_time[...], low)
    embeds = jnp.maximum(embeds, 0.0).astype(BF16)
    link = tn(w_link[0:width, :], embeds[:, :events]) + tn(w_link[width:, :], embeds[:, events:])
    high, low = split(jnp.maximum(link, 0.0))
    score = jnp.broadcast_to(w_score[...], (16, width))
    logits[...] = (nn(score, high) + nn(score, low))[0:1, :].astype(BF16)

    for q in range(4):
        await_all(4, msend, mrecv, max(q * 8, 1), q * 8 + 8)
        block = mrecv[q * 8 : (q + 1) * 8].reshape(512, LANES)
        part = tn(block, o_mat[q * 512 : (q + 1) * 512, :])
        s_acc[...] = part if q == 0 else s_acc[...] + part

    for j in range(4):
        at = slice(j * 256, (j + 1) * 256)
        count = time_part[336:337, at]
        inverse = 1.0 / jnp.maximum(count, 1.0)
        total = (nn(wg[1, 0:336, :], s_acc[:, at].astype(BF16)) + time_part[0:336, at]) * inverse + base[0:336, at]
        reset = sigmoid(total[0:112])
        update = sigmoid(total[112:224])
        candidate = jnp.tanh(total[224:336] + reset * base[336:448, at])
        handed = hrecv[:, at].astype(F32)
        updated = candidate + update * (handed - candidate)
        new_mem[:, at] = jnp.where(count > 0.0, updated, handed)[0:width, :].astype(BF16)

    hand.wait_send()

    def drain(d, c):
        for phase_no, src, dst in (
            (0, rsend, rrecv), (1, tsend, trecv), (2, ssend, srecv), (3, esend, erecv), (4, msend, mrecv),
        ):
            remote(phase_no, src, dst, d).wait_send()
        return c

    lax.fori_loop(1, PEERS, drain, 0)


def local_step(
    memory, embedding, owners, local_rows, event_slots, event_ticks,
    w_self, w_neighbour, w_time, w_link, w_score, w_message, w_hidden, frequencies, phases,
):
    nodes = memory.shape[2]
    events = event_slots.shape[2]
    args = (
        memory.reshape(-1, LANES),
        embedding,
        owners.reshape(-1, LANES),
        local_rows.reshape(-1, LANES),
        event_slots.transpose(1, 0, 2),
        event_ticks.transpose(1, 0, 2),
        w_self,
        w_neighbour,
        w_time,
        w_link.T,
        w_score.reshape(1, -1),
        w_message,
        w_hidden,
        frequencies.reshape(1, -1),
        phases.reshape(1, -1),
    )
    vmem = pl.BlockSpec(memory_space=pltpu.VMEM)
    block = (PEERS, CAP, LANES)
    scratch = [
        pltpu.VMEM((112, nodes), BF16),
        pltpu.VMEM((112, nodes), BF16),
        pltpu.VMEM((PEERS, 1, LANES), I32),
        pltpu.VMEM((PEERS, 1, LANES), I32),
        *[pltpu.VMEM(block, BF16)] * 8,
        pltpu.VMEM((LANES, 2 * events), BF16),
        pltpu.VMEM((104, 2 * events), F32),
        pltpu.VMEM((nodes, 2 * LANES), BF16),
        pltpu.VMEM((SLOTS, nodes), BF16),
        pltpu.VMEM((SLOTS, 2 * events), BF16),
        pltpu.VMEM((SLOTS, nodes), BF16),
        pltpu.VMEM((nodes, 2 * events), BF16),
        pltpu.VMEM((3, 352, LANES), BF16),
        pltpu.VMEM((336, 112), BF16),
        pltpu.VMEM((2, 112, 2 * LANES), BF16),
        pltpu.VMEM((448, nodes), F32),
        pltpu.VMEM((352, nodes), F32),
        pltpu.VMEM((LANES, 2 * events), F32),
        pltpu.VMEM((LANES, nodes), BF16),
        pltpu.VMEM((LANES, nodes), F32),
        pltpu.SemaphoreType.DMA((2,)),
        pltpu.SemaphoreType.DMA((5, PEERS)),
        pltpu.SemaphoreType.DMA((5, PEERS)),
    ]
    new_memory, logits = pl.pallas_call(
        kernel,
        out_shape=(
            jax.ShapeDtypeStruct((memory.shape[1], nodes), BF16),
            jax.ShapeDtypeStruct((1, events), BF16),
        ),
        in_specs=[vmem] * len(args),
        out_specs=(vmem, vmem),
        scratch_shapes=scratch,
        compiler_params=pltpu.CompilerParams(
            collective_id=0, has_side_effects=True, vmem_limit_bytes=56 * 1024 * 1024
        ),
    )(*args)
    return new_memory[None], logits


def solution(mesh):
    return jax.shard_map(
        local_step,
        mesh=mesh,
        in_specs=(
            P("group", None, "mem"),
            P(None, "mem"),
            P("group", "mem", None),
            P("group", "mem"),
            P("group", None, "mem"),
            P("group", None, "mem"),
            P(),
            P(),
            P(),
            P(),
            P(),
            P(),
            P(),
            P(),
            P(),
        ),
        out_specs=(P("group", None, "mem"), P("group", "mem")),
        check_vma=False,
    )
```

time: 55.5 us -> 50.6 us (0.912)
  Pallas kernels: 51 us -> 47.6 us
  local copies, waits for them, and re-layouts: 3.73 us -> 2.2 us
    pallas_call x1, Pallas kernels: 51 us -> 47.6 us  [local_step(): pl.pallas_call(kernel, out_shape=(jax.ShapeDtypeStruct((memory.shape[1],...]
    unnamed x5 -> x4, local copies, waits for them, and re-layouts: 3.73 us -> 2.2 us
where the time goes in v2:
time: 50.6 us; the launch traced here: 50.4 us
  Pallas kernels  47.6 us (94%)
  local copies, waits for them, and re-layouts  2.2 us (4%)
  between operations  0.65 us (1%)
    pallas_call x1, Pallas kernels, local_step(): pl.pallas_call(kernel, out_shape=(jax.ShapeDtypeStruct((memory.shape[1],...  47.6 us
    unnamed x4, local copies, waits for them, and re-layouts  2.2 us

profile of v2, /device:TPU:1, one launch (start us, length us, event | category | flops | bytes accessed | tf_op | source)
XLA Modules:
  0.0 50.4 jit_solution(15204087328758802444)
XLA Ops:
  0.6 47.6 %shard_map.158 = (bf16[100,1024]{1,0:T(8,128)(2,1)}, bf16[1,256]{1,0:T(2,128)(2,1)}) custom-call(f32[800,128]{1,0:T(8,128)} %bitcast.10, bf16[128,1024]{1,0:T(8,128)(2,1)} %emb.1, s32[8,128]{1,0:T(8,128)} %bitcast.15, s32[8,128]{1,0:T(8,128)} %bitcast.16, s32[22,1,256]{2,1,0:T(1,128)} %bitcast.13, s32[22,1,256]{2,1,0:T(1,128)} %bitcast.14, ...), custom_call_target="tpu_custom_call" | custom-call | tf_op jit(solution)/shard_map/pallas_call | solution.py:387
  48.2 0.0 copy-start
  48.2 1.6 %copy.19 = bf16[1,100,1024]{2,1,0:T(8,128)(2,1)} copy(bf16[1,100,1024]{2,1,0:T(8,128)(2,1)} %bitcast.11) | data formatting | bytes 409600
  49.9 0.0 copy-done
  49.9 0.6 %copy.20 = bf16[1,256]{1,0:T(2,128)(2,1)} copy(bf16[1,256]{1,0:T(2,128)(2,1)S(1)} %copy-done) | data formatting | bytes 1024
Async XLA Ops:
  48.2 1.6 %copy-start = (bf16[1,256]{1,0:T(2,128)(2,1)S(1)}, bf16[1,256]{1,0:T(2,128)(2,1)}, u32[]{:S(2)}) copy-start(bf16[1,256]{1,0:T(2,128)(2,1)} %get-tuple-element.9) | copy-start | bytes 1540

commit v3 on v2

--- a/solution.py
+++ b/solution.py
@@ -8,6 +8,7 @@
 MESH = pl.DeviceIdType.MESH
 F32, BF16, I32, I16 = jnp.float32, jnp.bfloat16, jnp.int32, jnp.int16
 PEERS, CAP, LANES = 32, 64, 128
+FIRST = 32
 SLOTS = PEERS * CAP
 TURN = 0.15915494309189535
 COS = (
@@ -79,12 +80,14 @@
 
 
 def kernel(
-    mem, emb, own, rows, slots, ticks, w_self, w_neigh, w_time, w_link, w_score, w_msg, w_hid, freq, phase,
+    mem_in, emb_in, own, rows, slots, ticks, w_self_in, w_neigh_in, w_time, w_link, w_score, w_msg_in, w_hid_in,
+    freq, phase,
     new_mem, logits,
+    mem, emb, w_self, w_neigh, w_msg, w_hid,
     hsend, hrecv, rsend, rrecv, esend, erecv, ssend, srecv, tsend, trecv, msend, mrecv,
-    codes, csum, table, o_mat, g_mat, p_mat, c_mat,
+    codes, csum, o_mat, g_mat, p_mat, c_mat,
     wg, wh, wp, base, time_part, self_acc, t_acc, s_acc,
-    hsem, send_sem, recv_sem,
+    in_sem, hsem, column_sem, send_sem, recv_sem,
 ):
     me = lax.axis_index("mem")
     group = lax.axis_index("group")
@@ -94,13 +97,21 @@
     width, events = 100, slots.shape[2]
 
     barrier = pltpu.get_barrier_semaphore()
+    columns = (8, 16, 24)
     pl.semaphore_signal(barrier, inc=1, device_id={"group": behind}, device_id_type=MESH)
-
-    def greet(d, c):
+    for d in (1, 2, 3, 4, 5, 6, 7, *columns):
         pl.semaphore_signal(barrier, inc=1, device_id={"mem": partner(me, d)}, device_id_type=MESH)
-        return c
-
-    lax.fori_loop(1, PEERS, greet, 0)
+    loads = [
+        pltpu.make_async_copy(src, dst, in_sem.at[i])
+        for i, (src, dst) in enumerate(
+            (
+                (mem_in, mem), (emb_in, emb), (w_self_in, w_self), (w_neigh_in, w_neigh), (w_msg_in, w_msg),
+                (w_hid_in, w_hid),
+            )
+        )
+    ]
+    for load in loads:
+        load.start()
 
     def remote(phase_no, src, dst, d):
         return pltpu.make_async_remote_copy(
@@ -126,6 +137,7 @@
 
         lax.fori_loop(low, high, go, 0)
 
+    loads[0].wait()
     for j in range(8):
         block = mem[pl.ds(j, width, stride=8), :]
         hsend[0:width, j * LANES : (j + 1) * LANES] = block.astype(BF16)
@@ -158,6 +170,21 @@
         rsend[d] = request[d : d + 1, :]
     rrecv[0] = request[0:1, :]
 
+    pl.semaphore_wait(barrier, 11)
+    hand = pltpu.make_async_remote_copy(
+        src_ref=hsend,
+        dst_ref=hrecv.at[0:112],
+        send_sem=hsem.at[0],
+        recv_sem=hsem.at[1],
+        device_id={"group": ahead},
+        device_id_type=MESH,
+    )
+    hand.start()
+    for d in columns:
+        pl.semaphore_signal(column_sem, inc=1, device_id={"mem": partner(me, d)}, device_id_type=MESH)
+    pl.semaphore_wait(column_sem, 3)
+    start_all(0, rsend, rrecv, 1, PEERS)
+
     refs = jnp.concatenate([slots[0], slots[1]], axis=1)
     sub8 = iota((16, 1024), 0)
     slot_parts = jnp.where(sub8 == 0, own_row.astype(F32), jnp.where(sub8 == 1, rank_row, 0.0)).astype(BF16)
@@ -186,22 +213,36 @@
     for d in range(PEERS):
         tsend[d] = sums[d * CAP : (d + 1) * CAP, :]
     trecv[0] = tsend[0]
-    table[:, LANES:] = emb[...].T
-
-    pl.semaphore_wait(barrier, PEERS)
-
-    hand = pltpu.make_async_remote_copy(
-        src_ref=hsend,
-        dst_ref=hrecv,
-        send_sem=hsem.at[0],
-        recv_sem=hsem.at[1],
-        device_id={"group": ahead},
-        device_id_type=MESH,
-    )
-    hand.start()
-    start_all(0, rsend, rrecv, 1, PEERS)
     start_all(1, tsend, trecv, 1, PEERS)
 
+    await_all(0, rsend, rrecv, 1, PEERS)
+    for p in range(PEERS // 2):
+        pair = jnp.where(iota((1, LANES), 1) < CAP, rrecv[2 * p], rrecv[2 * p + 1])
+        asked = column(pair.astype(F32)).astype(I32).astype(I16)
+        for j in range(8):
+            index = (iota((LANES, LANES), 1) + j * LANES).astype(I16)
+            o_mat[p * LANES : (p + 1) * LANES, j * LANES : (j + 1) * LANES] = jnp.where(
+                index == asked, jnp.ones((LANES, LANES), BF16), jnp.zeros((LANES, LANES), BF16)
+            )
+    def serve(rows_of, src, phase_no=None, dst=None):
+        for q in range(4):
+            got = nt(o_mat[q * 512 : (q + 1) * 512, :], rows_of[...]).astype(BF16)
+            for i in range(8):
+                src[q * 8 + i] = got[i * CAP : (i + 1) * CAP, :]
+            if dst is not None:
+                start_all(phase_no, src, dst, max(q * 8, 1), q * 8 + 8)
+
+    hand.wait_recv()
+    hrecv[112:128, :] = jnp.zeros((16, 1024), BF16)
+    serve(hrecv, ssend, 2, srecv)
+    srecv[0] = ssend[0]
+    loads[1].wait()
+    serve(emb, esend)
+    erecv[0] = esend[0]
+    start_all(3, esend, erecv, 1, FIRST)
+
+    for load in loads[2:]:
+        load.wait()
     wg[...] = jnp.zeros_like(wg)
     wh[...] = jnp.zeros_like(wh)
     wp[...] = jnp.zeros_like(wp)
@@ -241,30 +282,8 @@
             0, neighbours, add_code, jnp.zeros((104, events), F32)
         )
 
-    await_all(0, rsend, rrecv, 1, PEERS)
-    for p in range(PEERS // 2):
-        pair = jnp.where(iota((1, LANES), 1) < CAP, rrecv[2 * p], rrecv[2 * p + 1])
-        asked = column(pair.astype(F32)).astype(I32).astype(I16)
-        for j in range(8):
-            index = (iota((LANES, LANES), 1) + j * LANES).astype(I16)
-            o_mat[p * LANES : (p + 1) * LANES, j * LANES : (j + 1) * LANES] = jnp.where(
-                index == asked, jnp.ones((LANES, LANES), BF16), jnp.zeros((LANES, LANES), BF16)
-            )
-    hand.wait_recv()
-    table[:, 0:112] = hrecv[...].T
-    table[:, 112:128] = jnp.zeros((1024, 16), BF16)
-    for q in range(4):
-        got = nn(o_mat[q * 512 : (q + 1) * 512, :], table[...]).astype(BF16)
-        for i in range(8):
-            ssend[q * 8 + i] = got[i * CAP : (i + 1) * CAP, :LANES]
-            esend[q * 8 + i] = got[i * CAP : (i + 1) * CAP, LANES:]
-        start_all(2, ssend, srecv, max(q * 8, 1), q * 8 + 8)
-    start_all(3, esend, erecv, 1, PEERS)
-    srecv[0] = ssend[0]
-    erecv[0] = esend[0]
-
-    base[0:336, :] = nn(wg[0, 0:336, 0:112], hrecv[...])
-    hidden = nn(wh[...], hrecv[...])
+    base[0:336, :] = nn(wg[0, 0:336, 0:112], hrecv[0:112, :])
+    hidden = nn(wh[...], hrecv[0:112, :])
     base[0:224, :] = base[0:224, :] + hidden[0:224, :]
     base[336:448, :] = hidden[224:336, :]
 
@@ -280,6 +299,7 @@
         for i in range(8):
             msend[q * 8 + i] = sums[i * CAP : (i + 1) * CAP, :]
         start_all(4, msend, mrecv, max(q * 8, 1), q * 8 + 8)
+    start_all(3, esend, erecv, FIRST, PEERS)
     mrecv[0] = msend[0]
 
     await_all(1, tsend, trecv, 1, PEERS)
@@ -318,7 +338,7 @@
         reset = sigmoid(total[0:112])
         update = sigmoid(total[112:224])
         candidate = jnp.tanh(total[224:336] + reset * base[336:448, at])
-        handed = hrecv[:, at].astype(F32)
+        handed = hrecv[0:112, at].astype(F32)
         updated = candidate + update * (handed - candidate)
         new_mem[:, at] = jnp.where(count > 0.0, updated, handed)[0:width, :].astype(BF16)
 
@@ -332,6 +352,11 @@
         return c
 
     lax.fori_loop(1, PEERS, drain, 0)
+
+
+def hand_out(new_mem_in, logits_in, new_mem, logits):
+    new_mem[...] = new_mem_in[...]
+    logits[...] = logits_in[...]
 
 
 def local_step(
@@ -358,16 +383,17 @@
         phases.reshape(1, -1),
     )
     vmem = pl.BlockSpec(memory_space=pltpu.VMEM)
+    hbm = pl.BlockSpec(memory_space=pl.ANY)
     block = (PEERS, CAP, LANES)
     scratch = [
+        *[pltpu.VMEM(args[i].shape, args[i].dtype) for i in (0, 1, 6, 7, 11, 12)],
         pltpu.VMEM((112, nodes), BF16),
-        pltpu.VMEM((112, nodes), BF16),
+        pltpu.VMEM((LANES, nodes), BF16),
         pltpu.VMEM((PEERS, 1, LANES), I32),
         pltpu.VMEM((PEERS, 1, LANES), I32),
         *[pltpu.VMEM(block, BF16)] * 8,
         pltpu.VMEM((LANES, 2 * events), BF16),
         pltpu.VMEM((104, 2 * events), F32),
-        pltpu.VMEM((nodes, 2 * LANES), BF16),
         pltpu.VMEM((SLOTS, nodes), BF16),
         pltpu.VMEM((SLOTS, 2 * events), BF16),
         pltpu.VMEM((SLOTS, nodes), BF16),
@@ -380,7 +406,9 @@
         pltpu.VMEM((LANES, 2 * events), F32),
         pltpu.VMEM((LANES, nodes), BF16),
         pltpu.VMEM((LANES, nodes), F32),
+        pltpu.SemaphoreType.DMA((6,)),
         pltpu.SemaphoreType.DMA((2,)),
+        pltpu.SemaphoreType.REGULAR,
         pltpu.SemaphoreType.DMA((5, PEERS)),
         pltpu.SemaphoreType.DMA((5, PEERS)),
     ]
@@ -390,13 +418,22 @@
             jax.ShapeDtypeStruct((memory.shape[1], nodes), BF16),
             jax.ShapeDtypeStruct((1, events), BF16),
         ),
-        in_specs=[vmem] * len(args),
+        in_specs=[hbm if i in (0, 1, 6, 7, 11, 12) else vmem for i in range(len(args))],
         out_specs=(vmem, vmem),
         scratch_shapes=scratch,
         compiler_params=pltpu.CompilerParams(
             collective_id=0, has_side_effects=True, vmem_limit_bytes=56 * 1024 * 1024
         ),
     )(*args)
+    new_memory, logits = pl.pallas_call(
+        hand_out,
+        out_shape=(
+            jax.ShapeDtypeStruct((memory.shape[1], nodes), BF16),
+            jax.ShapeDtypeStruct((1, events), BF16),
+        ),
+        in_specs=[vmem, vmem],
+        out_specs=(vmem, vmem),
+    )(new_memory, logits)
     return new_memory[None], logits
 
 

time: 50.6 us -> 48 us (0.949)
  local copies, waits for them, and re-layouts: 2.2 us -> 0 us
    unnamed x4 -> x0, local copies, waits for them, and re-layouts: 2.2 us -> none
    pallas_call x1, Pallas kernels: 47.6 us -> 45.5 us  [local_step(): pl.pallas_call(kernel, out_shape=(jax.ShapeDtypeStruct((memory.shape[1],...]
    pallas_call x0 -> x1, Pallas kernels: none -> 1.64 us  [local_step(): pl.pallas_call(hand_out, out_shape=(jax.ShapeDtypeStruct((memory.shape[1]...]
where the time goes in v3:
time: 48 us; the launch traced here: 47.8 us
  Pallas kernels  47.2 us (98%)
  between operations  0.64 us (1%)
    pallas_call x1, Pallas kernels, local_step(): pl.pallas_call(kernel, out_shape=(jax.ShapeDtypeStruct((memory.shape[1],...  45.5 us
    pallas_call x1, Pallas kernels, local_step(): pl.pallas_call(hand_out, out_shape=(jax.ShapeDtypeStruct((memory.shape[1]...  1.64 us

profile of v3, /device:TPU:1, one launch (start us, length us, event | category | flops | bytes accessed | tf_op | source)
XLA Modules:
  0.0 47.8 jit_solution(5352074917282868617)
XLA Ops:
  0.6 45.5 %shard_map.158 = (bf16[100,1024]{1,0:T(8,128)(2,1)}, bf16[1,256]{1,0:T(2,128)(2,1)}) custom-call(f32[800,128]{1,0:T(8,128)} %bitcast.10, bf16[128,1024]{1,0:T(8,128)(2,1)} %emb_in.1, s32[8,128]{1,0:T(8,128)} %bitcast.14, s32[8,128]{1,0:T(8,128)} %bitcast.15, s32[22,1,256]{2,1,0:T(1,128)} %bitcast.12, s32[22,1,256]{2,1,0:T(1,128)} %bitcast.13, ...), custom_call_target="tpu_custom_call" | custom-call | tf_op jit(solution)/shard_map/pallas_call | solution.py:415
  46.2 1.6 %shard_map.159 = (bf16[100,1024]{1,0:T(8,128)(2,1)}, bf16[1,256]{1,0:T(2,128)(2,1)}) custom-call(bf16[100,1024]{1,0:T(8,128)(2,1)} %get-tuple-element.6.new_mem_in, bf16[1,256]{1,0:T(2,128)(2,1)} %get-tuple-element.7.logits_in), custom_call_target="tpu_custom_call" | custom-call | tf_op jit(solution)/shard_map/pallas_call | solution.py:428

commit v4 on v3

--- a/solution.py
+++ b/solution.py
@@ -8,7 +8,8 @@
 MESH = pl.DeviceIdType.MESH
 F32, BF16, I32, I16 = jnp.float32, jnp.bfloat16, jnp.int32, jnp.int16
 PEERS, CAP, LANES = 32, 64, 128
-FIRST = 32
+Y_ORDER = (2, 1, 3, 0)
+FAR_FIRST = [8 * y + x for y in Y_ORDER for x in (4, 5, 2, 3, 6, 7, 0, 1) if 8 * y + x > 0]
 SLOTS = PEERS * CAP
 TURN = 0.15915494309189535
 COS = (
@@ -79,16 +80,16 @@
     return out
 
 
-def kernel(
-    mem_in, emb_in, own, rows, slots, ticks, w_self_in, w_neigh_in, w_time, w_link, w_score, w_msg_in, w_hid_in,
-    freq, phase,
-    new_mem, logits,
-    mem, emb, w_self, w_neigh, w_msg, w_hid,
-    hsend, hrecv, rsend, rrecv, esend, erecv, ssend, srecv, tsend, trecv, msend, mrecv,
-    codes, csum, o_mat, g_mat, p_mat, c_mat,
-    wg, wh, wp, base, time_part, self_acc, t_acc, s_acc,
-    in_sem, hsem, column_sem, send_sem, recv_sem,
-):
+def kernel(*refs):
+    inputs, (new_mem_out, logits_out), held = refs[:15], refs[15:17], refs[17:32]
+    mem, emb, own, rows, slots, ticks, w_self, w_neigh, w_time, w_link, w_score, w_msg, w_hid, freq, phase = held
+    (
+        new_mem, logits,
+        hsend, hrecv, rsend, rmid, rrecv, esend, erecv, ssend, srecv, tsend, trecv, msend, mrecv,
+        codes, csum, o_mat, g_mat, p_mat, c_mat,
+        wg, wh, wp, base, time_part, self_acc, t_acc, s_acc,
+        in_sem, out_sem, hsem, column_sem, ask_sem, send_sem, recv_sem,
+    ) = refs[32:]
     me = lax.axis_index("mem")
     group = lax.axis_index("group")
     groups = lax.axis_size("group")
@@ -101,17 +102,10 @@
     pl.semaphore_signal(barrier, inc=1, device_id={"group": behind}, device_id_type=MESH)
     for d in (1, 2, 3, 4, 5, 6, 7, *columns):
         pl.semaphore_signal(barrier, inc=1, device_id={"mem": partner(me, d)}, device_id_type=MESH)
-    loads = [
-        pltpu.make_async_copy(src, dst, in_sem.at[i])
-        for i, (src, dst) in enumerate(
-            (
-                (mem_in, mem), (emb_in, emb), (w_self_in, w_self), (w_neigh_in, w_neigh), (w_msg_in, w_msg),
-                (w_hid_in, w_hid),
-            )
-        )
-    ]
-    for load in loads:
-        load.start()
+    loads = [pltpu.make_async_copy(src, dst, in_sem.at[i]) for i, (src, dst) in enumerate(zip(inputs, held))]
+    first, last = (2, 3, 0, 4, 5, 13, 14), (1, 6, 7, 8, 9, 10, 11, 12)
+    for i in first + last:
+        loads[i].start()
 
     def remote(phase_no, src, dst, d):
         return pltpu.make_async_remote_copy(
@@ -123,12 +117,9 @@
             device_id_type=MESH,
         )
 
-    def start_all(phase_no, src, dst, low, high):
-        def go(d, c):
+    def start_all(phase_no, src, dst, which):
+        for d in which:
             remote(phase_no, src, dst, d).start()
-            return c
-
-        lax.fori_loop(low, high, go, 0)
 
     def await_all(phase_no, src, dst, low, high):
         def go(d, c):
@@ -137,7 +128,8 @@
 
         lax.fori_loop(low, high, go, 0)
 
-    loads[0].wait()
+    for i in first:
+        loads[i].wait()
     for j in range(8):
         block = mem[pl.ds(j, width, stride=8), :]
         hsend[0:width, j * LANES : (j + 1) * LANES] = block.astype(BF16)
@@ -167,8 +159,8 @@
     member_row = hot_rows(own_row, PEERS)
     request = (nt(member_row, high_part) + nt(member_row, low_part)).astype(I32)
     for d in range(PEERS):
-        rsend[d] = request[d : d + 1, :]
-    rrecv[0] = request[0:1, :]
+        rsend[d // 8, d % 8] = request[d : d + 1, :]
+    rmid[0] = rsend[0]
 
     pl.semaphore_wait(barrier, 11)
     hand = pltpu.make_async_remote_copy(
@@ -180,10 +172,21 @@
         device_id_type=MESH,
     )
     hand.start()
+    down = [
+        pltpu.make_async_remote_copy(
+            src_ref=rsend.at[d // 8],
+            dst_ref=rmid.at[d // 8],
+            send_sem=ask_sem.at[0, d // 8],
+            recv_sem=ask_sem.at[1, d // 8],
+            device_id={"mem": partner(me, d)},
+            device_id_type=MESH,
+        )
+        for d in (16, 8, 24)
+    ]
+    for copy in down:
+        copy.start()
     for d in columns:
         pl.semaphore_signal(column_sem, inc=1, device_id={"mem": partner(me, d)}, device_id_type=MESH)
-    pl.semaphore_wait(column_sem, 3)
-    start_all(0, rsend, rrecv, 1, PEERS)
 
     refs = jnp.concatenate([slots[0], slots[1]], axis=1)
     sub8 = iota((16, 1024), 0)
@@ -213,36 +216,62 @@
     for d in range(PEERS):
         tsend[d] = sums[d * CAP : (d + 1) * CAP, :]
     trecv[0] = tsend[0]
-    start_all(1, tsend, trecv, 1, PEERS)
-
-    await_all(0, rsend, rrecv, 1, PEERS)
+    for copy in down:
+        copy.wait_recv()
+    along = [
+        pltpu.make_async_remote_copy(
+            src_ref=rmid.at[:, d],
+            dst_ref=rrecv.at[:, d],
+            send_sem=ask_sem.at[2, d],
+            recv_sem=ask_sem.at[3, d],
+            device_id={"mem": partner(me, d)},
+            device_id_type=MESH,
+        )
+        for d in (4, 5, 2, 3, 6, 7, 1)
+    ]
+    for copy in along:
+        copy.start()
+    for y in range(4):
+        rrecv[y, 0] = rmid[y, 0]
+    pl.semaphore_wait(column_sem, 3)
+    start_all(1, tsend, trecv, FAR_FIRST)
+
+    for copy in along:
+        copy.wait_recv()
     for p in range(PEERS // 2):
-        pair = jnp.where(iota((1, LANES), 1) < CAP, rrecv[2 * p], rrecv[2 * p + 1])
+        pair = jnp.where(iota((1, LANES), 1) < CAP, rrecv[p // 4, 2 * p % 8], rrecv[p // 4, 2 * p % 8 + 1])
         asked = column(pair.astype(F32)).astype(I32).astype(I16)
         for j in range(8):
             index = (iota((LANES, LANES), 1) + j * LANES).astype(I16)
             o_mat[p * LANES : (p + 1) * LANES, j * LANES : (j + 1) * LANES] = jnp.where(
                 index == asked, jnp.ones((LANES, LANES), BF16), jnp.zeros((LANES, LANES), BF16)
             )
-    def serve(rows_of, src, phase_no=None, dst=None):
-        for q in range(4):
+    def serve(rows_of, phase_no, src, dst):
+        for q in Y_ORDER:
             got = nt(o_mat[q * 512 : (q + 1) * 512, :], rows_of[...]).astype(BF16)
             for i in range(8):
                 src[q * 8 + i] = got[i * CAP : (i + 1) * CAP, :]
-            if dst is not None:
-                start_all(phase_no, src, dst, max(q * 8, 1), q * 8 + 8)
+            start_all(phase_no, src, dst, [d for d in FAR_FIRST if d // 8 == q])
+        dst[0] = src[0]
+
+    def serve_embedding():
+        loads[1].wait()
+        serve(emb, 3, esend, erecv)
+
+    @pl.when(group == 0)
+    def _():
+        serve_embedding()
 
     hand.wait_recv()
     hrecv[112:128, :] = jnp.zeros((16, 1024), BF16)
-    serve(hrecv, ssend, 2, srecv)
-    srecv[0] = ssend[0]
-    loads[1].wait()
-    serve(emb, esend)
-    erecv[0] = esend[0]
-    start_all(3, esend, erecv, 1, FIRST)
-
-    for load in loads[2:]:
-        load.wait()
+    serve(hrecv, 2, ssend, srecv)
+
+    @pl.when(group != 0)
+    def _():
+        serve_embedding()
+
+    for i in last[1:]:
+        loads[i].wait()
     wg[...] = jnp.zeros_like(wg)
     wh[...] = jnp.zeros_like(wh)
     wp[...] = jnp.zeros_like(wp)
@@ -287,19 +316,18 @@
     base[0:224, :] = base[0:224, :] + hidden[0:224, :]
     base[336:448, :] = hidden[224:336, :]
 
-    for q in range(4):
+    for q in Y_ORDER:
         await_all(2, ssend, srecv, max(q * 8, 1), q * 8 + 8)
         block = srecv[q * 8 : (q + 1) * 8].reshape(512, LANES)
         part = tn(block, g_mat[q * 512 : (q + 1) * 512, :])
-        self_acc[...] = part if q == 0 else self_acc[...] + part
+        self_acc[...] = part if q == Y_ORDER[0] else self_acc[...] + part
     self_state = self_acc[...].astype(BF16)
     other_state = jnp.concatenate([self_state[:, events:], self_state[:, :events]], axis=1)
-    for q in range(4):
+    for q in Y_ORDER:
         sums = nt(g_mat[q * 512 : (q + 1) * 512, :], other_state).astype(BF16)
         for i in range(8):
             msend[q * 8 + i] = sums[i * CAP : (i + 1) * CAP, :]
-        start_all(4, msend, mrecv, max(q * 8, 1), q * 8 + 8)
-    start_all(3, esend, erecv, FIRST, PEERS)
+        start_all(4, msend, mrecv, [d for d in FAR_FIRST if d // 8 == q])
     mrecv[0] = msend[0]
 
     await_all(1, tsend, trecv, 1, PEERS)
@@ -324,12 +352,16 @@
     score = jnp.broadcast_to(w_score[...], (16, width))
     logits[...] = (nn(score, high) + nn(score, low))[0:1, :].astype(BF16)
 
-    for q in range(4):
+    score_out = pltpu.make_async_copy(logits, logits_out, out_sem.at[4])
+    score_out.start()
+
+    for q in Y_ORDER:
         await_all(4, msend, mrecv, max(q * 8, 1), q * 8 + 8)
         block = mrecv[q * 8 : (q + 1) * 8].reshape(512, LANES)
         part = tn(block, o_mat[q * 512 : (q + 1) * 512, :])
-        s_acc[...] = part if q == 0 else s_acc[...] + part
-
+        s_acc[...] = part if q == Y_ORDER[0] else s_acc[...] + part
+
+    outs = []
     for j in range(4):
         at = slice(j * 256, (j + 1) * 256)
         count = time_part[336:337, at]
@@ -341,17 +373,24 @@
         handed = hrecv[0:112, at].astype(F32)
         updated = candidate + update * (handed - candidate)
         new_mem[:, at] = jnp.where(count > 0.0, updated, handed)[0:width, :].astype(BF16)
+        outs.append(pltpu.make_async_copy(new_mem.at[:, at], new_mem_out.at[:, at], out_sem.at[j]))
+        outs[j].start()
 
     hand.wait_send()
+    for copy in down + along:
+        copy.wait_send()
 
     def drain(d, c):
         for phase_no, src, dst in (
-            (0, rsend, rrecv), (1, tsend, trecv), (2, ssend, srecv), (3, esend, erecv), (4, msend, mrecv),
+            (1, tsend, trecv), (2, ssend, srecv), (3, esend, erecv), (4, msend, mrecv),
         ):
             remote(phase_no, src, dst, d).wait_send()
         return c
 
     lax.fori_loop(1, PEERS, drain, 0)
+    score_out.wait()
+    for copy in outs:
+        copy.wait()
 
 
 def hand_out(new_mem_in, logits_in, new_mem, logits):
@@ -386,11 +425,12 @@
     hbm = pl.BlockSpec(memory_space=pl.ANY)
     block = (PEERS, CAP, LANES)
     scratch = [
-        *[pltpu.VMEM(args[i].shape, args[i].dtype) for i in (0, 1, 6, 7, 11, 12)],
+        *[pltpu.VMEM(x.shape, x.dtype) for x in args],
+        pltpu.VMEM((memory.shape[1], nodes), BF16),
+        pltpu.VMEM((1, events), BF16),
         pltpu.VMEM((112, nodes), BF16),
         pltpu.VMEM((LANES, nodes), BF16),
-        pltpu.VMEM((PEERS, 1, LANES), I32),
-        pltpu.VMEM((PEERS, 1, LANES), I32),
+        *[pltpu.VMEM((4, 8, 1, LANES), I32)] * 3,
         *[pltpu.VMEM(block, BF16)] * 8,
         pltpu.VMEM((LANES, 2 * events), BF16),
         pltpu.VMEM((104, 2 * events), F32),
@@ -406,9 +446,11 @@
         pltpu.VMEM((LANES, 2 * events), F32),
         pltpu.VMEM((LANES, nodes), BF16),
         pltpu.VMEM((LANES, nodes), F32),
-        pltpu.SemaphoreType.DMA((6,)),
+        pltpu.SemaphoreType.DMA((15,)),
+        pltpu.SemaphoreType.DMA((5,)),
         pltpu.SemaphoreType.DMA((2,)),
         pltpu.SemaphoreType.REGULAR,
+        pltpu.SemaphoreType.DMA((4, 8)),
         pltpu.SemaphoreType.DMA((5, PEERS)),
         pltpu.SemaphoreType.DMA((5, PEERS)),
     ]
@@ -418,8 +460,8 @@
             jax.ShapeDtypeStruct((memory.shape[1], nodes), BF16),
             jax.ShapeDtypeStruct((1, events), BF16),
         ),
-        in_specs=[hbm if i in (0, 1, 6, 7, 11, 12) else vmem for i in range(len(args))],
-        out_specs=(vmem, vmem),
+        in_specs=[hbm] * len(args),
+        out_specs=(hbm, hbm),
         scratch_shapes=scratch,
         compiler_params=pltpu.CompilerParams(
             collective_id=0, has_side_effects=True, vmem_limit_bytes=56 * 1024 * 1024

time: 48 us -> 44.6 us (0.929)
  Pallas kernels: 47.2 us -> 43.9 us
    pallas_call x1, Pallas kernels: 45.5 us -> 42.2 us  [local_step(): pl.pallas_call(kernel, out_shape=(jax.ShapeDtypeStruct((memory.shape[1],...]
where the time goes in v4:
time: 44.6 us; the launch traced here: 44.5 us
  Pallas kernels  43.9 us (98%)
  between operations  0.64 us (1%)
    pallas_call x1, Pallas kernels, local_step(): pl.pallas_call(kernel, out_shape=(jax.ShapeDtypeStruct((memory.shape[1],...  42.2 us
    pallas_call x1, Pallas kernels, local_step(): pl.pallas_call(hand_out, out_shape=(jax.ShapeDtypeStruct((memory.shape[1]...  1.64 us

profile of v4, /device:TPU:1, one launch (start us, length us, event | category | flops | bytes accessed | tf_op | source)
XLA Modules:
  0.0 44.5 jit_solution(9698233816412109137)
XLA Ops:
  0.6 42.2 %shard_map.158 = (bf16[100,1024]{1,0:T(8,128)(2,1)}, bf16[1,256]{1,0:T(2,128)(2,1)}) custom-call(f32[800,128]{1,0:T(8,128)} %bitcast.10, bf16[128,1024]{1,0:T(8,128)(2,1)} %refs_1_.1, s32[8,128]{1,0:T(8,128)} %bitcast.14, s32[8,128]{1,0:T(8,128)} %bitcast.15, s32[22,1,256]{2,1,0:T(1,128)} %bitcast.12, s32[22,1,256]{2,1,0:T(1,128)} %bitcast.13, ...), custom_call_target="tpu_custom_call" | custom-call | tf_op jit(solution)/shard_map/pallas_call | solution.py:457
  42.9 1.6 %shard_map.159 = (bf16[100,1024]{1,0:T(8,128)(2,1)}, bf16[1,256]{1,0:T(2,128)(2,1)}) custom-call(bf16[100,1024]{1,0:T(8,128)(2,1)} %get-tuple-element.6.new_mem_in, bf16[1,256]{1,0:T(2,128)(2,1)} %get-tuple-element.7.logits_in), custom_call_target="tpu_custom_call" | custom-call | tf_op jit(solution)/shard_map/pallas_call | solution.py:470

commit v5 on v4

--- a/solution.py
+++ b/solution.py
@@ -10,7 +10,8 @@
 PEERS, CAP, LANES = 32, 64, 128
 Y_ORDER = (2, 1, 3, 0)
 FAR_FIRST = [8 * y + x for y in Y_ORDER for x in (4, 5, 2, 3, 6, 7, 0, 1) if 8 * y + x > 0]
-SLOTS = PEERS * CAP
+HALF = CAP // 2
+ROWS = PEERS * HALF
 TURN = 0.15915494309189535
 COS = (
     0.9999999890590219,
@@ -60,6 +61,14 @@
     return jnp.concatenate([jnp.where(index + jnp.int16(i) == named, one, zero) for i in range(0, count, 16)], axis=0)
 
 
+def swap(x):
+    return jnp.concatenate([x[:, CAP:], x[:, :CAP]], axis=1)
+
+
+def by_half(half, row):
+    return jnp.concatenate([jnp.where(half == 0, row, -1), jnp.where(half == 1, row, -1)], axis=1)
+
+
 def cos_turns(y):
     r = y - jnp.floor(y + 0.5)
     z = r * r
@@ -81,14 +90,14 @@
 
 
 def kernel(*refs):
-    inputs, (new_mem_out, logits_out), held = refs[:15], refs[15:17], refs[17:32]
+    inputs, (new_mem, logits), held = refs[:15], refs[15:17], refs[17:32]
     mem, emb, own, rows, slots, ticks, w_self, w_neigh, w_time, w_link, w_score, w_msg, w_hid, freq, phase = held
     (
-        new_mem, logits,
-        hsend, hrecv, rsend, rmid, rrecv, esend, erecv, ssend, srecv, tsend, trecv, msend, mrecv,
+        hsend, hrecv, rsend, rmid, rrecv, esend, erecv, tsend, trecv,
+        asend, arecv, bsend, brecv, masend, marecv, mbsend, mbrecv,
         codes, csum, o_mat, g_mat, p_mat, c_mat,
         wg, wh, wp, base, time_part, self_acc, t_acc, s_acc,
-        in_sem, out_sem, hsem, column_sem, ask_sem, send_sem, recv_sem,
+        in_sem, hsem, column_sem, ask_sem, send_sem, recv_sem,
     ) = refs[32:]
     me = lax.axis_index("mem")
     group = lax.axis_index("group")
@@ -97,13 +106,14 @@
     behind = lax.rem(group + groups - 1, groups)
     width, events = 100, slots.shape[2]
 
+    loads = [pltpu.make_async_copy(src, dst, in_sem.at[i]) for i, (src, dst) in enumerate(zip(inputs, held))]
+    first, last = (2, 3, 4, 5, 13, 14), (1, 6, 7, 8, 9, 10, 11, 12)
+    loads[0].start()
     barrier = pltpu.get_barrier_semaphore()
     columns = (8, 16, 24)
     pl.semaphore_signal(barrier, inc=1, device_id={"group": behind}, device_id_type=MESH)
     for d in (1, 2, 3, 4, 5, 6, 7, *columns):
         pl.semaphore_signal(barrier, inc=1, device_id={"mem": partner(me, d)}, device_id_type=MESH)
-    loads = [pltpu.make_async_copy(src, dst, in_sem.at[i]) for i, (src, dst) in enumerate(zip(inputs, held))]
-    first, last = (2, 3, 0, 4, 5, 13, 14), (1, 6, 7, 8, 9, 10, 11, 12)
     for i in first + last:
         loads[i].start()
 
@@ -128,13 +138,14 @@
 
         lax.fori_loop(low, high, go, 0)
 
-    for i in first:
-        loads[i].wait()
+    loads[0].wait()
     for j in range(8):
         block = mem[pl.ds(j, width, stride=8), :]
         hsend[0:width, j * LANES : (j + 1) * LANES] = block.astype(BF16)
     hsend[96:112, :] = jnp.where(iota((16, 1024), 0) < 4, hsend[96:112, :].astype(F32), 0.0).astype(BF16)
 
+    for i in first:
+        loads[i].wait()
     own_rel = own[...] ^ me
     local = rows[...]
     upper = iota((LANES, 2 * LANES), 0)
@@ -152,16 +163,48 @@
     own_row = jnp.concatenate([own_rel[r : r + 1, :] for r in range(8)], axis=1)
     local_row = jnp.concatenate([local[r : r + 1, :] for r in range(8)], axis=1)
     rank_int = rank_row.astype(I32)
-    in_rank = (iota((LANES, 1024), 0) & (CAP - 1)) == rank_int
+    place = iota((2 * LANES, 1024), 0)
+    in_rank = (place // LANES) * HALF + (place & (HALF - 1)) == rank_int
     local_low = local_row & 31
     high_part = jnp.where(in_rank, (local_row - local_low).astype(F32), 0.0).astype(BF16)
     low_part = jnp.where(in_rank, local_low.astype(F32), 0.0).astype(BF16)
     member_row = hot_rows(own_row, PEERS)
     request = (nt(member_row, high_part) + nt(member_row, low_part)).astype(I32)
     for d in range(PEERS):
-        rsend[d // 8, d % 8] = request[d : d + 1, :]
+        for h in range(2):
+            rsend[d // 8, d % 8, h : h + 1, :] = request[d : d + 1, h * LANES : (h + 1) * LANES]
     rmid[0] = rsend[0]
 
+    refs = jnp.concatenate([slots[0], slots[1]], axis=1)
+    sub8 = iota((16, 1024), 0)
+    slot_parts = jnp.where(sub8 == 0, own_row.astype(F32), jnp.where(sub8 == 1, rank_row, 0.0)).astype(BF16)
+    picked = nn(slot_parts, hot_rows(refs, 1024))
+    end_rank = picked[1:2, :].astype(I32)
+    end_row = picked[0:1, :].astype(I32) * HALF + (end_rank & (HALF - 1))
+    g_mat[...] = hot_rows(by_half(end_rank // HALF, end_row), ROWS)
+
+    pad = jnp.zeros((1, LANES - width), F32)
+    freq_col = column(jnp.concatenate([freq[...], pad], axis=1) * TURN)[0:104, :]
+    phase_col = column(jnp.concatenate([phase[...], pad], axis=1) * TURN)[0:104, :]
+
+    def code(k):
+        tick = ticks[k].astype(F32)
+        return jnp.concatenate(
+            [cos_turns(freq_col * tick[:, h * LANES : (h + 1) * LANES] + phase_col) for h in range(events // LANES)],
+            axis=1,
+        )
+
+    sub = iota((LANES, 2 * events), 0)
+    side = iota((LANES, 2 * events), 1) // events
+    ends = jnp.concatenate([code(0), code(1)], axis=1)
+    ends = jnp.concatenate([ends, jnp.zeros((LANES - 104, 2 * events), F32)], axis=0)
+    codes[...] = jnp.where(sub < width, ends, jnp.where(sub == width + side, 1.0, 0.0)).astype(BF16)
+
+    for h in range(2):
+        sums = nt(g_mat[:, h * 2 * events : (h + 1) * 2 * events], codes[...]).astype(BF16)
+        for d in range(PEERS):
+            tsend[d, h * HALF : (h + 1) * HALF] = sums[d * HALF : (d + 1) * HALF, :]
+    trecv[0] = tsend[0]
     pl.semaphore_wait(barrier, 11)
     hand = pltpu.make_async_remote_copy(
         src_ref=hsend,
@@ -188,34 +231,7 @@
     for d in columns:
         pl.semaphore_signal(column_sem, inc=1, device_id={"mem": partner(me, d)}, device_id_type=MESH)
 
-    refs = jnp.concatenate([slots[0], slots[1]], axis=1)
-    sub8 = iota((16, 1024), 0)
-    slot_parts = jnp.where(sub8 == 0, own_row.astype(F32), jnp.where(sub8 == 1, rank_row, 0.0)).astype(BF16)
-    picked = nn(slot_parts, hot_rows(refs, 1024))
-    end_slot = (picked[0:1, :] * float(CAP) + picked[1:2, :]).astype(I32)
-    g_mat[...] = hot_rows(end_slot, SLOTS)
-
-    pad = jnp.zeros((1, LANES - width), F32)
-    freq_col = column(jnp.concatenate([freq[...], pad], axis=1) * TURN)[0:104, :]
-    phase_col = column(jnp.concatenate([phase[...], pad], axis=1) * TURN)[0:104, :]
-
-    def code(k):
-        tick = ticks[k].astype(F32)
-        return jnp.concatenate(
-            [cos_turns(freq_col * tick[:, h * LANES : (h + 1) * LANES] + phase_col) for h in range(events // LANES)],
-            axis=1,
-        )
-
-    sub = iota((LANES, 2 * events), 0)
-    side = iota((LANES, 2 * events), 1) // events
-    ends = jnp.concatenate([code(0), code(1)], axis=1)
-    ends = jnp.concatenate([ends, jnp.zeros((LANES - 104, 2 * events), F32)], axis=0)
-    codes[...] = jnp.where(sub < width, ends, jnp.where(sub == width + side, 1.0, 0.0)).astype(BF16)
-
-    sums = nt(g_mat[...], codes[...]).astype(BF16)
-    for d in range(PEERS):
-        tsend[d] = sums[d * CAP : (d + 1) * CAP, :]
-    trecv[0] = tsend[0]
+    start_all(1, tsend, trecv, [d for d in FAR_FIRST if d < 8 or d in columns])
     for copy in down:
         copy.wait_recv()
     along = [
@@ -234,29 +250,38 @@
     for y in range(4):
         rrecv[y, 0] = rmid[y, 0]
     pl.semaphore_wait(column_sem, 3)
-    start_all(1, tsend, trecv, FAR_FIRST)
+    start_all(1, tsend, trecv, [d for d in FAR_FIRST if d >= 8 and d not in columns])
 
     for copy in along:
         copy.wait_recv()
-    for p in range(PEERS // 2):
-        pair = jnp.where(iota((1, LANES), 1) < CAP, rrecv[p // 4, 2 * p % 8], rrecv[p // 4, 2 * p % 8 + 1])
-        asked = column(pair.astype(F32)).astype(I32).astype(I16)
-        for j in range(8):
-            index = (iota((LANES, LANES), 1) + j * LANES).astype(I16)
-            o_mat[p * LANES : (p + 1) * LANES, j * LANES : (j + 1) * LANES] = jnp.where(
-                index == asked, jnp.ones((LANES, LANES), BF16), jnp.zeros((LANES, LANES), BF16)
+    quarter = iota((1, LANES), 1) // HALF
+    for p in range(PEERS // 4):
+        for h in range(2):
+            four = [rrecv[(4 * p + i) // 8, (4 * p + i) % 8, h : h + 1, :] for i in range(4)]
+            ask = jnp.where(
+                quarter < 2, jnp.where(quarter == 0, four[0], four[1]), jnp.where(quarter == 2, four[2], four[3])
             )
-    def serve(rows_of, phase_no, src, dst):
-        for q in Y_ORDER:
-            got = nt(o_mat[q * 512 : (q + 1) * 512, :], rows_of[...]).astype(BF16)
-            for i in range(8):
-                src[q * 8 + i] = got[i * CAP : (i + 1) * CAP, :]
-            start_all(phase_no, src, dst, [d for d in FAR_FIRST if d // 8 == q])
-        dst[0] = src[0]
+            asked = column(ask.astype(F32)).astype(I32).astype(I16)
+            for j in range(8):
+                index = (iota((LANES, LANES), 1) + j * LANES).astype(I16)
+                o_mat[p * LANES : (p + 1) * LANES, h * 1024 + j * LANES : h * 1024 + (j + 1) * LANES] = jnp.where(
+                    index == asked, jnp.ones((LANES, LANES), BF16), jnp.zeros((LANES, LANES), BF16)
+                )
+
+    def near_first(q):
+        return [d for d in FAR_FIRST if d // 8 == q]
+
+    def picked_rows(q, rows_of):
+        return [nt(o_mat[q * 256 : (q + 1) * 256, h * 1024 : (h + 1) * 1024], rows_of[...]) for h in range(2)]
 
     def serve_embedding():
         loads[1].wait()
-        serve(emb, 3, esend, erecv)
+        for q in Y_ORDER:
+            for h, got in enumerate(picked_rows(q, emb)):
+                for i in range(8):
+                    esend[q * 8 + i, h * HALF : (h + 1) * HALF] = got[i * HALF : (i + 1) * HALF, :].astype(BF16)
+            start_all(3, esend, erecv, near_first(q))
+        erecv[0] = esend[0]
 
     @pl.when(group == 0)
     def _():
@@ -264,7 +289,18 @@
 
     hand.wait_recv()
     hrecv[112:128, :] = jnp.zeros((16, 1024), BF16)
-    serve(hrecv, 2, ssend, srecv)
+    left = iota((256, LANES), 1) < CAP
+    for q in Y_ORDER:
+        first_half, second_half = picked_rows(q, hrecv)
+        low = jnp.where(left, first_half, swap(second_half)).astype(BF16)
+        high = jnp.where(left, swap(first_half), second_half).astype(BF16)
+        for i in range(8):
+            asend[q * 8 + i] = low[i * HALF : (i + 1) * HALF, :]
+            bsend[q * 8 + i] = high[i * HALF : (i + 1) * HALF, :]
+        start_all(2, asend, arecv, near_first(q))
+    start_all(5, bsend, brecv, FAR_FIRST)
+    arecv[0] = asend[0]
+    brecv[0] = bsend[0]
 
     @pl.when(group != 0)
     def _():
@@ -301,7 +337,7 @@
         for j in range(neighbours):
             total = total + jnp.where(index == near[j], one, zero)
         c_mat[q * 16 : (q + 1) * 16, :] = total
-    p_mat[...] = hot_rows(own_row * CAP + rank_int, SLOTS)
+    p_mat[...] = hot_rows(by_half(rank_int // HALF, own_row * HALF + (rank_int & (HALF - 1))), ROWS)
 
     for s in range(2):
         def add_code(j, total, s=s):
@@ -316,31 +352,50 @@
     base[0:224, :] = base[0:224, :] + hidden[0:224, :]
     base[336:448, :] = hidden[224:336, :]
 
-    for q in Y_ORDER:
-        await_all(2, ssend, srecv, max(q * 8, 1), q * 8 + 8)
-        block = srecv[q * 8 : (q + 1) * 8].reshape(512, LANES)
-        part = tn(block, g_mat[q * 512 : (q + 1) * 512, :])
-        self_acc[...] = part if q == Y_ORDER[0] else self_acc[...] + part
-    self_state = self_acc[...].astype(BF16)
-    other_state = jnp.concatenate([self_state[:, events:], self_state[:, :events]], axis=1)
-    for q in Y_ORDER:
-        sums = nt(g_mat[q * 512 : (q + 1) * 512, :], other_state).astype(BF16)
-        for i in range(8):
-            msend[q * 8 + i] = sums[i * CAP : (i + 1) * CAP, :]
-        start_all(4, msend, mrecv, [d for d in FAR_FIRST if d // 8 == q])
-    mrecv[0] = msend[0]
-
     await_all(1, tsend, trecv, 1, PEERS)
-    t_acc[...] = tn(trecv[...].reshape(SLOTS, LANES), o_mat[...]).astype(BF16)
+    t_acc[...] = sum(
+        tn(trecv[:, h * HALF : (h + 1) * HALF, :].reshape(ROWS, LANES), o_mat[:, h * 1024 : (h + 1) * 1024])
+        for h in range(2)
+    ).astype(BF16)
     time_part[...] = nn(wg[2], t_acc[...])
 
+    self_parts = []
+    wide = 2 * events
+    for got_no, sent_no, src, dst, out, back in (
+        (2, 4, asend, arecv, masend, marecv),
+        (5, 6, bsend, brecv, mbsend, mbrecv),
+    ):
+        for q in Y_ORDER:
+            await_all(got_no, src, dst, max(q * 8, 1), q * 8 + 8)
+            block = dst[q * 8 : (q + 1) * 8].reshape(256, LANES)
+            part = tn(block, g_mat[q * 256 : (q + 1) * 256, :])
+            self_acc[...] = part if q == Y_ORDER[0] else self_acc[...] + part
+        own_part = (self_acc[0:CAP, 0:wide] + self_acc[CAP:LANES, wide:]).astype(BF16)
+        self_parts.append(own_part)
+        turned = jnp.concatenate([own_part[:, events:], own_part[:, :events]], axis=1)
+        blank = jnp.zeros((CAP, wide), BF16)
+        packed = jnp.concatenate(
+            [jnp.concatenate([turned, blank], axis=1), jnp.concatenate([blank, turned], axis=1)], axis=0
+        )
+        for q in Y_ORDER:
+            sums = nt(g_mat[q * 256 : (q + 1) * 256, :], packed).astype(BF16)
+            for i in range(8):
+                out[q * 8 + i] = sums[i * HALF : (i + 1) * HALF, :]
+            start_all(sent_no, out, back, near_first(q))
+        back[0] = out[0]
+    self_state = jnp.concatenate(self_parts, axis=0)
+
     await_all(3, esend, erecv, 1, PEERS)
-    embed_all = erecv[...].reshape(SLOTS, LANES)
-    fetched_state = tn(srecv[...].reshape(SLOTS, LANES), p_mat[...]).astype(BF16)
-    fetched_embed = tn(embed_all, p_mat[...]).astype(BF16)
+    left = iota((ROWS, LANES), 1) < CAP
+    low, high = arecv[...].reshape(ROWS, LANES).astype(F32), brecv[...].reshape(ROWS, LANES).astype(F32)
+    state_rows = jnp.where(left, low, swap(high)).astype(BF16), jnp.where(left, swap(low), high).astype(BF16)
+    embed_rows = [erecv[:, h * HALF : (h + 1) * HALF, :].reshape(ROWS, LANES) for h in range(2)]
+    spread = [p_mat[:, h * 1024 : (h + 1) * 1024] for h in range(2)]
+    fetched_state = (tn(state_rows[0], spread[0]) + tn(state_rows[1], spread[1])).astype(BF16)
+    fetched_embed = (tn(embed_rows[0], spread[0]) + tn(embed_rows[1], spread[1])).astype(BF16)
     near_state = nn(fetched_state, c_mat[...])
     near_embed = nn(fetched_embed, c_mat[...])
-    self_embed = tn(embed_all, g_mat[...]).astype(BF16)
+    self_embed = (tn(embed_rows[0], g_mat[:, :wide]) + tn(embed_rows[1], g_mat[:, wide:])).astype(BF16)
     pre = nn(wp[0], jnp.concatenate([self_state, self_embed], axis=0))
     for half in split(jnp.concatenate([near_state, near_embed], axis=0)):
         pre = pre + nn(wp[1], half)
@@ -352,16 +407,16 @@
     score = jnp.broadcast_to(w_score[...], (16, width))
     logits[...] = (nn(score, high) + nn(score, low))[0:1, :].astype(BF16)
 
-    score_out = pltpu.make_async_copy(logits, logits_out, out_sem.at[4])
-    score_out.start()
-
+    await_all(4, masend, marecv, 1, PEERS)
+    total = tn(marecv[...].reshape(ROWS, LANES), o_mat[...])
+    s_acc[0:CAP, :] = total[0:CAP, 0:1024] + total[CAP:LANES, 1024:2048]
     for q in Y_ORDER:
-        await_all(4, msend, mrecv, max(q * 8, 1), q * 8 + 8)
-        block = mrecv[q * 8 : (q + 1) * 8].reshape(512, LANES)
-        part = tn(block, o_mat[q * 512 : (q + 1) * 512, :])
-        s_acc[...] = part if q == Y_ORDER[0] else s_acc[...] + part
-
-    outs = []
+        await_all(6, mbsend, mbrecv, max(q * 8, 1), q * 8 + 8)
+        block = mbrecv[q * 8 : (q + 1) * 8].reshape(256, LANES)
+        part = tn(block, o_mat[q * 256 : (q + 1) * 256, :])
+        part = part[0:CAP, 0:1024] + part[CAP:LANES, 1024:2048]
+        s_acc[CAP:LANES, :] = part if q == Y_ORDER[0] else s_acc[CAP:LANES, :] + part
+
     for j in range(4):
         at = slice(j * 256, (j + 1) * 256)
         count = time_part[336:337, at]
@@ -373,8 +428,6 @@
         handed = hrecv[0:112, at].astype(F32)
         updated = candidate + update * (handed - candidate)
         new_mem[:, at] = jnp.where(count > 0.0, updated, handed)[0:width, :].astype(BF16)
-        outs.append(pltpu.make_async_copy(new_mem.at[:, at], new_mem_out.at[:, at], out_sem.at[j]))
-        outs[j].start()
 
     hand.wait_send()
     for copy in down + along:
@@ -382,20 +435,13 @@
 
     def drain(d, c):
         for phase_no, src, dst in (
-            (1, tsend, trecv), (2, ssend, srecv), (3, esend, erecv), (4, msend, mrecv),
+            (1, tsend, trecv), (2, asend, arecv), (3, esend, erecv), (4, masend, marecv), (5, bsend, brecv),
+            (6, mbsend, mbrecv),
         ):
             remote(phase_no, src, dst, d).wait_send()
         return c
 
     lax.fori_loop(1, PEERS, drain, 0)
-    score_out.wait()
-    for copy in outs:
-        copy.wait()
-
-
-def hand_out(new_mem_in, logits_in, new_mem, logits):
-    new_mem[...] = new_mem_in[...]
-    logits[...] = logits_in[...]
 
 
 def local_step(
@@ -423,59 +469,47 @@
     )
     vmem = pl.BlockSpec(memory_space=pltpu.VMEM)
     hbm = pl.BlockSpec(memory_space=pl.ANY)
-    block = (PEERS, CAP, LANES)
     scratch = [
         *[pltpu.VMEM(x.shape, x.dtype) for x in args],
-        pltpu.VMEM((memory.shape[1], nodes), BF16),
-        pltpu.VMEM((1, events), BF16),
         pltpu.VMEM((112, nodes), BF16),
         pltpu.VMEM((LANES, nodes), BF16),
-        *[pltpu.VMEM((4, 8, 1, LANES), I32)] * 3,
-        *[pltpu.VMEM(block, BF16)] * 8,
+        *[pltpu.VMEM((4, 8, 2, LANES), I32)] * 3,
+        *[pltpu.VMEM((PEERS, CAP, LANES), BF16)] * 4,
+        *[pltpu.VMEM((PEERS, HALF, LANES), BF16)] * 8,
         pltpu.VMEM((LANES, 2 * events), BF16),
         pltpu.VMEM((104, 2 * events), F32),
-        pltpu.VMEM((SLOTS, nodes), BF16),
-        pltpu.VMEM((SLOTS, 2 * events), BF16),
-        pltpu.VMEM((SLOTS, nodes), BF16),
+        pltpu.VMEM((ROWS, 2 * nodes), BF16),
+        pltpu.VMEM((ROWS, 4 * events), BF16),
+        pltpu.VMEM((ROWS, 2 * nodes), BF16),
         pltpu.VMEM((nodes, 2 * events), BF16),
         pltpu.VMEM((3, 352, LANES), BF16),
         pltpu.VMEM((336, 112), BF16),
         pltpu.VMEM((2, 112, 2 * LANES), BF16),
         pltpu.VMEM((448, nodes), F32),
         pltpu.VMEM((352, nodes), F32),
-        pltpu.VMEM((LANES, 2 * events), F32),
+        pltpu.VMEM((LANES, 4 * events), F32),
         pltpu.VMEM((LANES, nodes), BF16),
         pltpu.VMEM((LANES, nodes), F32),
         pltpu.SemaphoreType.DMA((15,)),
-        pltpu.SemaphoreType.DMA((5,)),
         pltpu.SemaphoreType.DMA((2,)),
         pltpu.SemaphoreType.REGULAR,
         pltpu.SemaphoreType.DMA((4, 8)),
-        pltpu.SemaphoreType.DMA((5, PEERS)),
-        pltpu.SemaphoreType.DMA((5, PEERS)),
+        pltpu.SemaphoreType.DMA((7, PEERS)),
+        pltpu.SemaphoreType.DMA((7, PEERS)),
     ]
     new_memory, logits = pl.pallas_call(
         kernel,
         out_shape=(
-            jax.ShapeDtypeStruct((memory.shape[1], nodes), BF16),
-            jax.ShapeDtypeStruct((1, events), BF16),
+            pltpu.VMEM((memory.shape[1], nodes), BF16),
+            pltpu.VMEM((1, events), BF16),
         ),
-        in_specs=[hbm] * len(args),
-        out_specs=(hbm, hbm),
+        in_specs=[pl.BlockSpec(memory_space=pltpu.HBM)] * len(args),
+        out_specs=(vmem, vmem),
         scratch_shapes=scratch,
         compiler_params=pltpu.CompilerParams(
             collective_id=0, has_side_effects=True, vmem_limit_bytes=56 * 1024 * 1024
         ),
     )(*args)
-    new_memory, logits = pl.pallas_call(
-        hand_out,
-        out_shape=(
-            jax.ShapeDtypeStruct((memory.shape[1], nodes), BF16),
-            jax.ShapeDtypeStruct((1, events), BF16),
-        ),
-        in_specs=[vmem, vmem],
-        out_specs=(vmem, vmem),
-    )(new_memory, logits)
     return new_memory[None], logits
 
 

time: 44.6 us -> 44.1 us (0.989)
  Pallas kernels: 43.9 us -> 42.1 us
  local copies, waits for them, and re-layouts: 0 us -> 1.25 us
    pallas_call x2 -> x1, Pallas kernels: 43.9 us -> 42.1 us  [local_step(): pl.pallas_call(kernel, out_shape=(pltpu.VMEM((memory.shape[1], nodes), BF...]
    unnamed x0 -> x2, local copies, waits for them, and re-layouts: none -> 1.25 us
where the time goes in v5:
time: 44.1 us; the launch traced here: 44 us
  Pallas kernels  42.1 us (95%)
  local copies, waits for them, and re-layouts  1.25 us (3%)
  between operations  0.65 us (1%)
    pallas_call x1, Pallas kernels, local_step(): pl.pallas_call(kernel, out_shape=(pltpu.VMEM((memory.shape[1], nodes), BF...  42.1 us
    unnamed x2, local copies, waits for them, and re-layouts  1.25 us

profile of v5, /device:TPU:1, one launch (start us, length us, event | category | flops | bytes accessed | tf_op | source)
XLA Modules:
  0.0 44.0 jit_solution(5346184654256468575)
XLA Ops:
  0.6 42.1 %shard_map.158 = (bf16[100,1024]{1,0:T(8,128)(2,1)S(1)}, bf16[1,256]{1,0:T(2,128)(2,1)S(1)}) custom-call(f32[800,128]{1,0:T(8,128)} %bitcast.11, bf16[128,1024]{1,0:T(8,128)(2,1)} %refs_1_.1, s32[8,128]{1,0:T(8,128)} %bitcast.15, s32[8,128]{1,0:T(8,128)} %bitcast.16, s32[22,1,256]{2,1,0:T(1,128)} %bitcast.13, s32[22,1,256]{2,1,0:T(1,128)} %bitcast.14, ...), custom_call_target="tpu_custom_call" | custom-call | tf_op jit(solution)/shard_map/pallas_call | solution.py:500
  42.7 0.7 %copy.19 = bf16[1,100,1024]{2,1,0:T(8,128)(2,1)} copy(bf16[1,100,1024]{2,1,0:T(8,128)(2,1)S(1)} %bitcast.10) | data formatting | bytes 409600
  43.4 0.6 %copy.20 = bf16[1,256]{1,0:T(2,128)(2,1)} copy(bf16[1,256]{1,0:T(2,128)(2,1)S(1)} %get-tuple-element.7) | data formatting | bytes 1024
